TPU v7x, 256 devices: a whole 4x4x8 slice. The times are simulated.
256 devices in a mesh: hx: 16 (over z, y_hi), hy: 8 (over x, core), ga: 2 (over y_lo).
Axes of the slice: x: 4, y: 4 (y_hi: 2, y_lo: 2; y = y_hi * 2 + y_lo), z: 8, core: 2. Of those that a mesh axis runs over, the one named last changes fastest.
Arguments:
- density: float32 [128, 256, 256], P('hx', 'hy', 'ga'), may hold values from 0.5 to 2
- velocity: float32 [3, 128, 256, 256], P(None, 'hx', 'hy', 'ga'), may hold values from -3 to 3
- pressure: float32 [128, 256, 256], P('hx', 'hy', 'ga'), may hold values from 0.3 to 3
- species: float32 [9, 128, 256, 256], P(None, 'hx', 'hy', 'ga'), may hold values from 0.05 to 1
- newton_count: int32 [128, 256, 256], P('hx', 'hy', 'ga'), may hold values from 1 to 4
Outputs:
- new_density: float32 [128, 256, 256], P('hx', 'hy', 'ga')
- momentum: float32 [3, 128, 256, 256], P(None, 'hx', 'hy', 'ga')
- total_energy: float32 [128, 256, 256], P('hx', 'hy', 'ga')
- species_mass: float32 [9, 128, 256, 256], P(None, 'hx', 'hy', 'ga')
- potential: float32 [128, 256, 256], P('hx', 'hy', 'ga')
Inputs may be any that keep to these rules, and one draw needn't show every extreme that they name: `newton_count`: how many Newton iterations each cell takes.
All inputs are finite; a program needn't handle non-finite values.
Results may differ from a plain program's by a relative error of at most 0.0003.
Values sent between devices are 32-bit elements; how exact they have to be, the bound alone decides.
A program may use at most 128 MiB of HBM per device.

v0:
```python
import jax
import jax.numpy as jnp
from jax import lax
from jax.sharding import PartitionSpec as P

NEWTON = 4


gamma_gas = 5.0 / 3.0
time_step = 0.1
cool_rates = (2.0, 5.0, 9.0, 14.0, 20.0, 3.0, 7.0, 11.0, 29.0)
highest = lax.Precision.HIGHEST


def extended(cells, sides, width):
    for axis, dim in sides:
        count = lax.axis_size(axis)
        head = lax.slice_in_dim(cells, 0, width, axis=dim)
        tail = lax.slice_in_dim(cells, cells.shape[dim] - width, cells.shape[dim], axis=dim)
        cells = jnp.concatenate(
            [
                lax.ppermute(tail, axis, [(i, (i + 1) % count) for i in range(count)]),
                cells,
                lax.ppermute(head, axis, [((i + 1) % count, i) for i in range(count)]),
            ],
            axis=dim,
        )
    return cells


def cooled_pressure(density, pressure, species, newton_count):
    cooling = cool_rates[0] * species[0]
    for species_index in range(1, 9):
        cooling = cooling + cool_rates[species_index] * species[species_index]
    stiffness = time_step * density * cooling
    initial = pressure / ((gamma_gas - 1.0) * density)
    energy = initial
    for newton_step in range(NEWTON):
        residual_value = energy - initial + stiffness * energy * energy / (1.0 + energy)
        derivative = 1.0 + stiffness * energy * (energy + 2.0) / ((1.0 + energy) * (1.0 + energy))
        energy = jnp.where(newton_count > newton_step, energy - residual_value / derivative, energy)
    return (gamma_gas - 1.0) * density * energy


def conserved(primitive):
    density = primitive[0]
    velocity = primitive[1:4]
    kinetic = (
        0.5
        * density
        * (velocity[0] * velocity[0] + velocity[1] * velocity[1] + velocity[2] * velocity[2])
    )
    energy = primitive[4] / (gamma_gas - 1.0) + kinetic
    return jnp.concatenate(
        [density[None], density[None] * velocity, energy[None], density[None] * primitive[5:14]],
        axis=0,
    )


def face_flux(lower_cells, upper_cells, direction):
    sides_data = []
    for side_cells in (lower_cells, upper_cells):
        amounts = conserved(side_cells)
        normal = side_cells[1 + direction]
        carried = amounts * normal[None]
        carried = carried.at[1 + direction].add(side_cells[4])
        carried = carried.at[4].add(side_cells[4] * normal)
        signal = jnp.abs(normal) + jnp.sqrt(gamma_gas * side_cells[4] / side_cells[0])
        sides_data.append((amounts, carried, signal))
    wave_speed = jnp.maximum(sides_data[0][2], sides_data[1][2])
    return 0.5 * (sides_data[0][1] + sides_data[1][1]) - 0.5 * wave_speed[None] * (
        sides_data[1][0] - sides_data[0][0]
    )


def window(padded, array_axis, offset, extent):
    selection = [slice(None), slice(1, -1), slice(1, -1), slice(1, -1)]
    selection[array_axis] = slice(offset, offset + extent)
    return padded[tuple(selection)]


def advance(padded):
    primitive = padded[0:14]
    current = conserved(primitive[:, 1:-1, 1:-1, 1:-1])
    change = jnp.zeros_like(current)
    accelerations = []
    for direction in range(3):
        array_axis = 1 + direction
        extent = current.shape[array_axis]
        across = face_flux(
            window(primitive, array_axis, 0, extent + 1),
            window(primitive, array_axis, 1, extent + 1),
            direction,
        )
        change = change + (
            lax.slice_in_dim(across, 1, extent + 1, axis=array_axis)
            - lax.slice_in_dim(across, 0, extent, axis=array_axis)
        )
        accelerations.append(
            -0.5
            * (
                window(padded[14:15], array_axis, 2, extent)
                - window(padded[14:15], array_axis, 0, extent)
            )[0]
        )
    updated = current - time_step * change
    density = current[0]
    momentum = jnp.concatenate(
        [
            (updated[1 + direction] + time_step * density * accelerations[direction])[None]
            for direction in range(3)
        ],
        axis=0,
    )
    energy = updated[4] + time_step * (
        current[1] * accelerations[0]
        + current[2] * accelerations[1]
        + current[3] * accelerations[2]
    )
    return (updated[0], momentum, energy, updated[5:14])


def hartley(row_keys, col_keys, length):
    phase = row_keys[:, None] * col_keys[None, :] % length
    angle = 2.0 * jnp.pi / length * phase.astype(jnp.float32)
    return jnp.cos(angle) + jnp.sin(angle)


def eigen_keys(keys, extent):
    return 2.0 * jnp.cos(2.0 * jnp.pi / extent * keys.astype(jnp.float32)) - 2.0


def spectral_solve(planes_data, wave_y, total_y):
    total_x = planes_data.shape[0]
    total_z = planes_data.shape[2]
    keys_x = jnp.arange(total_x, dtype=jnp.int32)
    keys_z = jnp.arange(total_z, dtype=jnp.int32)
    table_x = hartley(keys_x, keys_x, total_x)
    table_z = hartley(keys_z, keys_z, total_z)
    turned = jnp.einsum("ab,byz->ayz", table_x, planes_data, precision=highest)
    turned = jnp.einsum("ayz,zc->ayc", turned, table_z, precision=highest)
    total = (
        eigen_keys(keys_x, total_x)[:, None, None]
        + eigen_keys(wave_y, total_y)[None, :, None]
        + eigen_keys(keys_z, total_z)[None, None, :]
    )
    green = jnp.where(total < 0.0, 1.0 / jnp.where(total < 0.0, total, -1.0), 0.0) / (
        total_x * total_y * total_z
    )
    turned = turned * green
    turned = jnp.einsum("ab,byz->ayz", table_x, turned, precision=highest)
    return jnp.einsum("ayz,zc->ayc", turned, table_z, precision=highest)


def column_pass(field, table):
    turned = jnp.einsum(
        "ab,xbz->xaz",
        table,
        lax.all_to_all(field, "hy", split_axis=0, concat_axis=1, tiled=True),
        precision=highest,
    )
    return lax.all_to_all(turned, "hy", split_axis=1, concat_axis=0, tiled=True)


def local(density, velocity, pressure, species, newton_count):
    size_x = lax.axis_size("hx")
    size_y = lax.axis_size("hy")
    size_g = lax.axis_size("ga")
    rank_x = lax.axis_index("hx")
    rank_y = lax.axis_index("hy")
    rank_g = lax.axis_index("ga")
    rows_y = density.shape[1]
    total_y = rows_y * size_y
    slab_share = rows_y // size_x
    thin_rows = slab_share // size_g
    keys_y = jnp.arange(total_y, dtype=jnp.int32)
    local_keys = jnp.arange(thin_rows, dtype=jnp.int32)
    table_y = hartley(keys_y, keys_y, total_y)
    spectral = column_pass(density, table_y)
    planes_data = lax.all_to_all(
        lax.all_to_all(spectral, "hx", split_axis=1, concat_axis=0, tiled=True),
        "ga",
        split_axis=1,
        concat_axis=2,
        tiled=True,
    )
    wave_y = (rank_y * size_x + rank_x) * slab_share + rank_g * thin_rows + local_keys
    solved = spectral_solve(planes_data, wave_y, total_y)
    returned = lax.all_to_all(
        lax.all_to_all(solved, "hx", split_axis=0, concat_axis=1, tiled=True),
        "ga",
        split_axis=2,
        concat_axis=1,
        tiled=True,
    )
    source_block = keys_y // rows_y
    inner_pos = keys_y % rows_y
    from_group = inner_pos // (thin_rows * size_x)
    remainder = inner_pos % (thin_rows * size_x)
    column_keys = (
        source_block * rows_y
        + remainder // thin_rows * slab_share
        + from_group * thin_rows
        + remainder % thin_rows
    )
    potential = column_pass(returned, hartley(keys_y, column_keys, total_y))
    cooled = cooled_pressure(density, pressure, species, newton_count)
    gas_stack = jnp.concatenate(
        [density[None], velocity, cooled[None], species, potential[None]], axis=0
    )
    padded = extended(gas_stack, (("hx", 1), ("hy", 2), ("ga", 3)), 1)
    new_density, momentum, total_energy, species_mass = advance(padded)
    return (new_density, momentum, total_energy, species_mass, potential)


def solution(mesh):
    in_specs = (
        P("hx", "hy", "ga"),
        P(None, "hx", "hy", "ga"),
        P("hx", "hy", "ga"),
        P(None, "hx", "hy", "ga"),
        P("hx", "hy", "ga"),
    )
    out_specs = (
        P("hx", "hy", "ga"),
        P(None, "hx", "hy", "ga"),
        P("hx", "hy", "ga"),
        P(None, "hx", "hy", "ga"),
        P("hx", "hy", "ga"),
    )
    return jax.shard_map(local, mesh=mesh, in_specs=in_specs, out_specs=out_specs, check_vma=False)
```

profile of v0, /device:TPU:1, one launch (start us, length us, event | category | flops | bytes accessed | tf_op | source)
XLA Modules:
  0.0 211.3 jit_solution(15273414521462295522)
XLA Ops:
  0.6 11.9 %all_to_all.108 = f32[8,32,128]{2,1,0:T(8,128)S(1)} all-to-all(f32[8,32,128]{2,1,0:T(8,128)} %param.29), channel_id=1, replica_groups=mesh['hx'=16,'hy'=8,'ga'=2] {'hy'}, dimensions={0} | all-to-all | bytes 262144 | tf_op jit(solution)/shard_map/all_to_all | solution.py:159
  14.2 8.5 %all_to_all.109 = f32[1,256,128]{2,0,1:T(1,128)S(1)} all-to-all(f32[1,256,128]{2,0,1:T(1,128)S(1)} %bitcast.119), channel_id=1, replica_groups=mesh['hx'=16,'hy'=8,'ga'=2] {'hy'}, dimensions={1} | all-to-all | bytes 262144 | tf_op jit(solution)/shard_map/all_to_all | solution.py:162
  23.5 10.3 %all-to-all-start.2 = ((f32[8,32,128]{2,0,1:T(8,128)}), f32[8,32,128]{2,0,1:T(8,128)}, u32[]{:S(2)}, u32[]{:S(2)}) async-start(f32[8,32,128]{2,0,1:T(8,128)} %copy.131), calls=%async_computation.2 | async-start | bytes 262144 | tf_op jit(solution)/shard_map/all_to_all | solution.py:181
  36.7 7.1 %all-to-all-done.2 = f32[8,32,128]{2,0,1:T(8,128)} async-done(((f32[8,32,128]{2,0,1:T(8,128)}), f32[8,32,128]{2,0,1:T(8,128)}, u32[]{:S(2)}, u32[]{:S(2)}) %all-to-all-start.2) | async-done | bytes 131104 | tf_op jit(solution)/shard_map/all_to_all | solution.py:181
  45.3 4.0 %all-to-all-start.3 = ((f32[128,2,128]{2,0,1:T(8,128)}), f32[128,2,128]{2,0,1:T(8,128)}, u32[]{:S(2)}, u32[]{:S(2)}) async-start(f32[128,2,128]{2,0,1:T(8,128)} %bitcast.117), calls=%async_computation.3 | async-start | bytes 262144 | tf_op jit(solution)/shard_map/all_to_all | solution.py:180
  49.4 3.4 %all-to-all-done.3 = f32[128,2,128]{2,0,1:T(8,128)} async-done(((f32[128,2,128]{2,0,1:T(8,128)}), f32[128,2,128]{2,0,1:T(8,128)}, u32[]{:S(2)}, u32[]{:S(2)}) %all-to-all-start.3) | async-done | bytes 131104 | tf_op jit(solution)/shard_map/all_to_all | solution.py:180
  59.9 4.2 %all-to-all-start.4 = ((f32[128,1,256]{2,1,0:T(1,128)}), f32[128,1,256]{2,1,0:T(1,128)}, u32[]{:S(2)}, u32[]{:S(2)}) async-start(f32[128,1,256]{2,1,0:T(1,128)} %copy.134), calls=%async_computation.4 | async-start | bytes 262144 | tf_op jit(solution)/shard_map/all_to_all | solution.py:190
  66.2 7.9 %all-to-all-done.4 = f32[128,1,256]{2,1,0:T(1,128)} async-done(((f32[128,1,256]{2,1,0:T(1,128)}), f32[128,1,256]{2,1,0:T(1,128)}, u32[]{:S(2)}, u32[]{:S(2)}) %all-to-all-start.4) | async-done | bytes 131104 | tf_op jit(solution)/shard_map/all_to_all | solution.py:190
  80.9 4.0 %all-to-all-start.5 = ((f32[2,1,16384]{2,1,0:T(1,128)}), f32[2,1,16384]{2,1,0:T(1,128)}, u32[]{:S(2)}, u32[]{:S(2)}) async-start(f32[2,1,16384]{2,1,0:T(1,128)} %reshape.580), calls=%async_computation.5 | async-start | bytes 262144 | tf_op jit(solution)/shard_map/all_to_all | solution.py:189
  97.5 9.6 %all-to-all-start.6 = ((f32[8,32,128]{2,1,0:T(8,128)}), f32[8,32,128]{2,1,0:T(8,128)}, u32[]{:S(2)}, u32[]{:S(2)}) async-start(f32[8,32,128]{2,1,0:T(8,128)} %bitcast.116), calls=%async_computation.6 | async-start | bytes 262144 | tf_op jit(solution)/shard_map/all_to_all | solution.py:159
  108.0 4.5 %all-to-all-done.6 = f32[8,32,128]{2,1,0:T(8,128)} async-done(((f32[8,32,128]{2,1,0:T(8,128)}), f32[8,32,128]{2,1,0:T(8,128)}, u32[]{:S(2)}, u32[]{:S(2)}) %all-to-all-start.6) | async-done | bytes 131104 | tf_op jit(solution)/shard_map/all_to_all | solution.py:159
  112.5 3.0 %convolution_bitcast_fusion = f32[1,256,128]{1,2,0:T(8,128)} fusion(f32[256,128]{1,0:T(8,128)} %bitcast.22, s32[256]{0:T(256)S(1)} %fusion.138), kind=kOutput, calls=%fused_computation.53 | convolution fusion | flops 101646336 | bytes 263168 | tf_op jit(solution)/shard_map/ab,xbz->xaz/dot_general | solution.py:156
  117.1 4.7 %all-to-all-start.7 = ((f32[1,256,128]{2,0,1:T(1,128)}), f32[1,256,128]{2,0,1:T(1,128)}, u32[]{:S(2)}, u32[]{:S(2)}) async-start(f32[1,256,128]{2,0,1:T(1,128)} %copy.138), calls=%async_computation.7 | async-start | bytes 262144 | tf_op jit(solution)/shard_map/all_to_all | solution.py:162
  123.7 3.6 %all-to-all-done.7 = f32[1,256,128]{2,0,1:T(1,128)} async-done(((f32[1,256,128]{2,0,1:T(1,128)}), f32[1,256,128]{2,0,1:T(1,128)}, u32[]{:S(2)}, u32[]{:S(2)}) %all-to-all-start.7) | async-done | bytes 131104 | tf_op jit(solution)/shard_map/all_to_all | solution.py:162
  129.1 4.8 %collective-permute-start.1 = (f32[15,1,32,128]{3,1,2,0:T(1,128)S(1)}, f32[15,1,32,128]{3,1,2,0:T(1,128)S(1)}, u32[]{:S(2)}, u32[]{:S(2)}) collective-permute-start(f32[15,1,32,128]{3,1,2,0:T(1,128)S(1)} %get-tuple-element.218), channel_id=1, source_target_pairs={{16,0},{32,16},{48,32},{64,48},{80,64},{96,80},{112,96},{128,112},... | collective-permute-start | bytes 737288 | tf_op jit(solution)/shard_map/ppermute | solution.py:24
  133.8 5.2 %collective-permute-done = f32[15,1,32,128]{3,1,2,0:T(1,128)S(1)} collective-permute-done((f32[15,1,32,128]{3,1,2,0:T(1,128)S(1)}, f32[15,1,32,128]{3,1,2,0:T(1,128)S(1)}, u32[]{:S(2)}, u32[]{:S(2)}) %collective-permute-start) | collective-permute-done | bytes 245792 | tf_op jit(solution)/shard_map/ppermute | solution.py:22
  139.0 3.1 %collective-permute-done.1 = f32[15,1,32,128]{3,1,2,0:T(1,128)S(1)} collective-permute-done((f32[15,1,32,128]{3,1,2,0:T(1,128)S(1)}, f32[15,1,32,128]{3,1,2,0:T(1,128)S(1)}, u32[]{:S(2)}, u32[]{:S(2)}) %collective-permute-start.1) | collective-permute-done | bytes 245792 | tf_op jit(solution)/shard_map/ppermute | solution.py:24
  159.6 4.7 %fusion.166 = (f32[15,10,34,1]{3,1,2,0:T(8,128)}, f32[15,10,34,1]{3,1,2,0:T(8,128)}) fusion(f32[15,10,34,128]{3,1,2,0:T(8,128)S(1)} %pad_maximum_fusion), kind=kLoop, calls=%fused_computation.323 | loop fusion | bytes 81600 | tf_op jit(solution)/shard_map/slice | solution.py:18
  164.4 4.2 %copy.148 = f32[15,10,34,1]{2,0,3,1:T(8,128)} copy(f32[15,10,34,1]{3,1,2,0:T(8,128)} %get-tuple-element.197) | data formatting | bytes 40800 | tf_op jit(solution)/shard_map/slice | solution.py:19
  168.6 4.2 %copy.155 = f32[15,10,34,1]{2,0,3,1:T(8,128)} copy(f32[15,10,34,1]{3,1,2,0:T(8,128)} %get-tuple-element.196) | data formatting | bytes 40800 | tf_op jit(solution)/shard_map/slice | solution.py:18
  174.2 4.6 %multiply_subtract_fusion.2 = f32[14,8,33,128]{3,1,2,0:T(8,128)} fusion(f32[14,8,33,128]{3,1,2,0:T(8,128)} %fusion.78, f32[14,8,33,128]{3,1,2,0:T(8,128)} %copy-done.4, f32[9,8,33,128]{3,1,2,0:T(8,128)} %copy-done.2, f32[1,8,33,128]{3,1,2,0:T(8,128)} %copy-done.12, f32[3,8,33,128]{3,1,2,0:T(8,128)S(1)} %get-tuple-element.202, ...), kind=kLoop, calls=%fused_computation.43 | loop fusion | flops 5203968 | bytes 9596928 | tf_op jit(solution)/shard_map/sub | solution.py:71
  178.8 4.1 %copy.149 = f32[15,10,34,1]{3,1,2,0:T(8,128)} copy(f32[15,10,34,1]{2,0,3,1:T(8,128)} %collective-permute-done.4) | data formatting | bytes 40800 | tf_op jit(solution)/shard_map/ppermute | solution.py:22
  182.9 4.1 %copy.156 = f32[15,10,34,1]{3,1,2,0:T(8,128)} copy(f32[15,10,34,1]{2,0,3,1:T(8,128)} %collective-permute-done.5) | data formatting | bytes 40800 | tf_op jit(solution)/shard_map/ppermute | solution.py:24
  199.1 6.7 %fusion.10 = f32[14,8,32,128]{3,1,2,0:T(8,128)S(1)} fusion(f32[14,8,32,129]{3,1,2,0:T(8,128)} %multiply_subtract_fusion, f32[14,8,33,128]{3,1,2,0:T(8,128)} %multiply_subtract_fusion.2, f32[14,9,32,128]{3,1,2,0:T(8,128)} %multiply_subtract_fusion.1, f32[9,8,32,128]{3,1,2,0:T(8,128)} %get-tuple-element.220, f32[1,8,32,128]{3,1,2,0:T(8,128)S(1)} %copy-done.13, ...), kind=kLoop, calls=%fused_computation.47 | loop fusion | flops 4587520 | bytes 14680064 | tf_op jit(solution)/shard_map/sub | solution.py:106
  (114 shorter events, 77.8 us)
Async XLA Ops:
  0.6 34.1 %copy-start.5 = (f32[9,8,32,128]{3,2,1,0:T(8,128)S(1)}, f32[9,8,32,128]{3,2,1,0:T(8,128)}, u32[]{:S(2)}) copy-start(f32[9,8,32,128]{3,2,1,0:T(8,128)} %param.32) | copy-start | bytes 3538948
  12.6 24.0 %copy-start.8 = (f32[8,32,128]{2,1,0:T(8,128)S(1)}, f32[8,32,128]{2,1,0:T(8,128)}, u32[]{:S(2)}) copy-start(f32[8,32,128]{2,1,0:T(8,128)} %param.29) | copy-start | bytes 393220
  23.5 20.3 %all-to-all-start.2 = ((f32[8,32,128]{2,0,1:T(8,128)}), f32[8,32,128]{2,0,1:T(8,128)}, u32[]{:S(2)}, u32[]{:S(2)}) async-start(f32[8,32,128]{2,0,1:T(8,128)} %copy.131), calls=%async_computation.2 | async-start | bytes 262144 | tf_op jit(solution)/shard_map/all_to_all | solution.py:181
  34.8 87.1 %copy-start.9 = (f32[8,32,128]{2,0,1:T(8,128)}, f32[8,32,128]{2,0,1:T(8,128)S(1)}, u32[]{:S(2)}) copy-start(f32[8,32,128]{2,0,1:T(8,128)S(1)} %copy.199) | copy-start | bytes 393220
  45.3 7.4 %all-to-all-start.3 = ((f32[128,2,128]{2,0,1:T(8,128)}), f32[128,2,128]{2,0,1:T(8,128)}, u32[]{:S(2)}, u32[]{:S(2)}) async-start(f32[128,2,128]{2,0,1:T(8,128)} %bitcast.117), calls=%async_computation.3 | async-start | bytes 262144 | tf_op jit(solution)/shard_map/all_to_all | solution.py:180
  59.9 14.2 %all-to-all-start.4 = ((f32[128,1,256]{2,1,0:T(1,128)}), f32[128,1,256]{2,1,0:T(1,128)}, u32[]{:S(2)}, u32[]{:S(2)}) async-start(f32[128,1,256]{2,1,0:T(1,128)} %copy.134), calls=%async_computation.4 | async-start | bytes 262144 | tf_op jit(solution)/shard_map/all_to_all | solution.py:190
  80.9 7.4 %all-to-all-start.5 = ((f32[2,1,16384]{2,1,0:T(1,128)}), f32[2,1,16384]{2,1,0:T(1,128)}, u32[]{:S(2)}, u32[]{:S(2)}) async-start(f32[2,1,16384]{2,1,0:T(1,128)} %reshape.580), calls=%async_computation.5 | async-start | bytes 262144 | tf_op jit(solution)/shard_map/all_to_all | solution.py:189
  97.5 15.0 %all-to-all-start.6 = ((f32[8,32,128]{2,1,0:T(8,128)}), f32[8,32,128]{2,1,0:T(8,128)}, u32[]{:S(2)}, u32[]{:S(2)}) async-start(f32[8,32,128]{2,1,0:T(8,128)} %bitcast.116), calls=%async_computation.6 | async-start | bytes 262144 | tf_op jit(solution)/shard_map/all_to_all | solution.py:159
  117.1 10.1 %all-to-all-start.7 = ((f32[1,256,128]{2,0,1:T(1,128)}), f32[1,256,128]{2,0,1:T(1,128)}, u32[]{:S(2)}, u32[]{:S(2)}) async-start(f32[1,256,128]{2,0,1:T(1,128)} %copy.138), calls=%async_computation.7 | async-start | bytes 262144 | tf_op jit(solution)/shard_map/all_to_all | solution.py:162
  128.7 10.3 %collective-permute-start = (f32[15,1,32,128]{3,1,2,0:T(1,128)S(1)}, f32[15,1,32,128]{3,1,2,0:T(1,128)S(1)}, u32[]{:S(2)}, u32[]{:S(2)}) collective-permute-start(f32[15,1,32,128]{3,1,2,0:T(1,128)S(1)} %get-tuple-element.217), channel_id=1, source_target_pairs={{0,16},{16,32},{32,48},{48,64},{64,80},{80,96},{96,112},{112,128},... | collective-permute-start | bytes 737288 | tf_op jit(solution)/shard_map/ppermute | solution.py:22
  129.1 13.1 %collective-permute-start.1 = (f32[15,1,32,128]{3,1,2,0:T(1,128)S(1)}, f32[15,1,32,128]{3,1,2,0:T(1,128)S(1)}, u32[]{:S(2)}, u32[]{:S(2)}) collective-permute-start(f32[15,1,32,128]{3,1,2,0:T(1,128)S(1)} %get-tuple-element.218), channel_id=1, source_target_pairs={{16,0},{32,16},{48,32},{64,48},{80,64},{96,80},{112,96},{128,112},... | collective-permute-start | bytes 737288 | tf_op jit(solution)/shard_map/ppermute | solution.py:24
  144.8 4.8 %collective-permute-start.2 = (f32[15,10,1,128]{3,0,2,1:T(8,128)S(1)}, f32[15,10,1,128]{3,0,2,1:T(8,128)S(1)}, u32[]{:S(2)}, u32[]{:S(2)}) collective-permute-start(f32[15,10,1,128]{3,0,2,1:T(8,128)S(1)} %copy.142), channel_id=1, source_target_pairs={{0,2},{2,4},{4,6},{6,8},{8,10},{10,12},{12,14},{14,0},{1,3},{3,5},... | collective-permute-start | bytes 230408 | tf_op jit(solution)/shard_map/ppermute | solution.py:22
  147.1 4.2 %collective-permute-start.3 = (f32[15,10,1,128]{3,0,2,1:T(8,128)S(1)}, f32[15,10,1,128]{3,0,2,1:T(8,128)S(1)}, u32[]{:S(2)}, u32[]{:S(2)}) collective-permute-start(f32[15,10,1,128]{3,0,2,1:T(8,128)S(1)} %copy.144), channel_id=1, source_target_pairs={{2,0},{4,2},{6,4},{8,6},{10,8},{12,10},{14,12},{0,14},{3,1},{5,3},... | collective-permute-start | bytes 230408 | tf_op jit(solution)/shard_map/ppermute | solution.py:24
  152.5 1.4 copy-start.3
  152.6 2.9 %copy-start.11 = (f32[1,8,33,128]{3,1,2,0:T(8,128)}, f32[1,8,33,128]{3,1,2,0:T(8,128)S(1)}, u32[]{:S(2)}) copy-start(f32[1,8,33,128]{3,1,2,0:T(8,128)S(1)} %fusion.82) | copy-start | bytes 405508
  152.7 2.8 %copy-start.12 = (f32[1,8,33,128]{3,1,2,0:T(8,128)}, f32[1,8,33,128]{3,1,2,0:T(8,128)S(1)}, u32[]{:S(2)}) copy-start(f32[1,8,33,128]{3,1,2,0:T(8,128)S(1)} %fusion.76) | copy-start | bytes 405508
  155.6 1.7 copy-start.4
  168.6 10.2 %collective-permute-start.4 = (f32[15,10,34,1]{2,0,3,1:T(8,128)}, f32[15,10,34,1]{2,0,3,1:T(8,128)}, u32[]{:S(2)}, u32[]{:S(2)}) collective-permute-start(f32[15,10,34,1]{2,0,3,1:T(8,128)} %copy.148), channel_id=1, source_target_pairs={{0,1},{1,0},{2,3},{3,2},{4,5},{5,4},{6,7},{7,6},{8,9},{9,8},{10,11... | collective-permute-start | bytes 61208 | tf_op jit(solution)/shard_map/ppermute | solution.py:22
  172.7 10.2 %collective-permute-start.5 = (f32[15,10,34,1]{2,0,3,1:T(8,128)}, f32[15,10,34,1]{2,0,3,1:T(8,128)}, u32[]{:S(2)}, u32[]{:S(2)}) collective-permute-start(f32[15,10,34,1]{2,0,3,1:T(8,128)} %copy.155), channel_id=1, source_target_pairs={{1,0},{0,1},{3,2},{2,3},{5,4},{4,5},{7,6},{6,7},{9,8},{8,9},{11,10... | collective-permute-start | bytes 61208 | tf_op jit(solution)/shard_map/ppermute | solution.py:24
  187.1 2.7 %copy-start = (f32[15,10,34,1]{3,1,2,0:T(8,128)S(1)}, f32[15,10,34,1]{3,1,2,0:T(8,128)}, u32[]{:S(2)}) copy-start(f32[15,10,34,1]{3,1,2,0:T(8,128)} %copy.149) | copy-start | bytes 61204
  187.1 3.9 %copy-start.1 = (f32[15,10,34,1]{3,1,2,0:T(8,128)S(1)}, f32[15,10,34,1]{3,1,2,0:T(8,128)}, u32[]{:S(2)}) copy-start(f32[15,10,34,1]{3,1,2,0:T(8,128)} %copy.156) | copy-start | bytes 61204
  196.2 2.9 %copy-start.7 = (f32[3,8,32,128]{3,1,2,0:T(8,128)S(1)}, f32[3,8,32,128]{3,1,2,0:T(8,128)}, u32[]{:S(2)}) copy-start(f32[3,8,32,128]{3,1,2,0:T(8,128)} %get-tuple-element.222) | copy-start | bytes 1179652
  196.2 2.8 %copy-start.10 = (f32[8,32,128]{2,0,1:T(8,128)S(1)}, f32[8,32,128]{2,0,1:T(8,128)}, u32[]{:S(2)}) copy-start(f32[8,32,128]{2,0,1:T(8,128)} %copy-done.9) | copy-start | bytes 393220
  196.2 2.8 %copy-start.13 = (f32[1,8,32,128]{3,1,2,0:T(8,128)S(1)}, f32[1,8,32,128]{3,1,2,0:T(8,128)}, u32[]{:S(2)}) copy-start(f32[1,8,32,128]{3,1,2,0:T(8,128)} %get-tuple-element.173) | copy-start | bytes 393220
  (2 other events, 1.8 us)
where the time goes:
time: 213 us; the launch traced here: 211 us
  local copies, waits for them, and re-layouts  54.5 us (26%)
  starting transfers between devices  45.7 us (21%)
  other arithmetic  43.3 us (20%)
  waiting for transfers between devices  37 us (17%)
  blocking collectives  20.4 us (10%)
  matrix products  9.23 us (4%)
    unnamed x40, local copies, waits for them, and re-layouts  18.6 us
    all_to_all x1, blocking collectives, column_pass(): lax.all_to_all(field, 'hy', split_axis=0, concat_axis=1, tiled=True)  11.9 us
    all_to_all x1, starting transfers between devices, local(): lax.all_to_all(spectral, 'hx', split_axis=1, concat_axis=0, tiled=True)  10.3 us
    sub x3, other arithmetic, face_flux(): 0.5 * (sides_data[0][1] + sides_data[1][1])  9.85 us
    all_to_all x1, starting transfers between devices, column_pass(): lax.all_to_all(field, 'hy', split_axis=0, concat_axis=1, tiled=True)  9.61 us
    slice x3, local copies, waits for them, and re-layouts, extended(): head = lax.slice_in_dim(cells, 0, width, axis=dim)  8.95 us
    all_to_all x1, blocking collectives, column_pass(): return lax.all_to_all(turned, 'hy', split_axis=1, concat_axis=0, tiled=True)  8.52 us
    all_to_all x1, waiting for transfers between devices, local(): lax.all_to_all(solved, 'hx', split_axis=0, concat_axis=1, tiled=True)  7.92 us
  transfers between devices with their start and end apart: 12, of which 9 were waited for; matrix products, arithmetic and copies ran while one was open for 12% of the time, Pallas kernels for 0%

commit v1 on v0

v1 whole, which is shorter than its diff:
```python
import functools

import jax
import jax.numpy as jnp
import ml_dtypes
import numpy as np
from jax import lax
from jax.experimental import pallas as pl
from jax.experimental.pallas import tpu as pltpu
from jax.sharding import PartitionSpec as P

NEWTON = 4
gamma_gas = 5.0 / 3.0
time_step = 0.1
half_step = 0.5 * time_step
cool_rates = (2.0, 5.0, 9.0, 14.0, 20.0, 3.0, 7.0, 11.0, 29.0)
NX, NY, NZ = 128, 256, 256
BX, BY, BZ = 8, 32, 128
MESH = pl.DeviceIdType.MESH
f32 = jnp.float32
bf16 = jnp.bfloat16


def cas_table(length):
    keys = np.arange(length)
    angle = 2.0 * np.pi / length * (keys[:, None] * keys[None, :] % length)
    return np.cos(angle) + np.sin(angle)


def halves(table):
    table = table.astype(np.float32)
    high = table.astype(ml_dtypes.bfloat16)
    low = (table - high.astype(np.float32)).astype(ml_dtypes.bfloat16)
    return np.stack([high, low])


def eigen(extent):
    waves = np.arange(extent).astype(np.float32)
    return np.float32(2.0) * np.cos(np.float32(2.0 * np.pi / extent) * waves) - np.float32(2.0)


def tables():
    table_y = cas_table(NY)
    table_z = cas_table(NZ)
    parts = []
    for rank in range(NZ // BZ):
        first = rank * BZ
        edges = np.zeros((NZ, BZ))
        edges[:, 0] = table_z[:, (first - 1) % NZ]
        edges[:, BZ - 1] = table_z[:, (first + BZ) % NZ]
        parts.append(halves(np.concatenate([table_z[:, first : first + BZ], edges], axis=1)))
    lam_xy = (eigen(NX)[:, None] + eigen(NY)[None, :]).astype(np.float32)
    return np.stack(parts), halves(table_y), halves(cas_table(NX)), lam_xy, eigen(NZ).astype(np.float32)


def split(values):
    high = values.astype(bf16)
    return high, (values - high.astype(f32)).astype(bf16)


def dot3(left, right, dims=(((1,), (0,)), ((), ()))):
    def one(i, j):
        return lax.dot_general(left[i], right[j], dims, preferred_element_type=f32)

    return one(0, 0) + (one(0, 1) + one(1, 0))


def swap_chunks(tiles, lane):
    low = lane < 64
    even = (lane // 32) % 2 == 0
    mid = [None] * 4
    for i in range(2):
        mid[i] = jnp.where(low, tiles[i], pltpu.roll(tiles[i + 2], 64, 1))
        mid[i + 2] = jnp.where(low, pltpu.roll(tiles[i], 64, 1), tiles[i + 2])
    out = [None] * 4
    for i in (0, 2):
        out[i] = jnp.where(even, mid[i], pltpu.roll(mid[i + 1], 32, 1))
        out[i + 1] = jnp.where(even, pltpu.roll(mid[i], 96, 1), mid[i + 1])
    return out


def kernel(
    density, velocity, pressure, species, counts, tz_in, ty_in, tx_in, lam_in, lamz,
    o_density, o_momentum, o_energy, o_species, o_potential,
    gas, sound, press, count, tz, ty, tx, lam, out, pot,
    z_src, z_buf, u_buf, y_src, x_buf, x_src, w_buf, v_buf, b_src, b_buf,
    yp_src, yp_buf, zp_src, zp_buf, py_src, py_buf,
    in_sem, out_sem, send_sem, recv_sem, halo_send, halo_recv,
):
    a = lax.axis_index("hx")
    b = lax.axis_index("hy")
    g = lax.axis_index("ga")
    q = g * 8 + b

    loads = [
        (density, gas.at[0, pl.ds(1, BX)]),
        (tz_in.at[g], tz),
        (velocity, gas.at[pl.ds(1, 3), pl.ds(1, BX)]),
        (species, gas.at[pl.ds(5, 9), pl.ds(1, BX)]),
        (pressure, press),
        (counts, count),
        (ty_in, ty),
        (tx_in, tx),
        (lam_in, lam),
    ]
    loads = [pltpu.make_async_copy(s, d, in_sem.at[i]) for i, (s, d) in enumerate(loads)]
    for load in loads:
        load.start()

    barrier = pltpu.get_barrier_semaphore()

    def plane_id(offset):
        t = lax.rem(q + offset, 16)
        return t, {"hy": lax.rem(t, 8), "ga": t // 8}

    def line_id(offset):
        t = lax.rem(a + offset, 16)
        return t, {"hx": t}

    @pl.loop(1, 16)
    def _(d):
        pl.semaphore_signal(barrier, inc=1, device_id=plane_id(d)[1], device_id_type=MESH)
        pl.semaphore_signal(barrier, inc=1, device_id=line_id(d)[1], device_id_type=MESH)

    def remote(src, dst, sems, slot, target):
        return pltpu.make_async_remote_copy(
            src_ref=src, dst_ref=dst, send_sem=sems[0].at[slot], recv_sem=sems[1].at[slot],
            device_id=target, device_id_type=MESH,
        )

    rounds = [(send_sem.at[r], recv_sem.at[r]) for r in range(4)]

    def send1(d):
        t, where = plane_id(d)
        return remote(z_src.at[:, pl.ds(t * 16, 16)], z_buf.at[q], rounds[0], d, where)

    def send2(d):
        t, where = line_id(d)
        return remote(y_src.at[pl.ds(t * 8, 8)], x_buf.at[pl.ds(a * 8, 8)], rounds[1], d, where)

    def send3(d):
        t, where = line_id(d)
        return remote(x_src.at[pl.ds(t * 8, 8)], w_buf.at[pl.ds(a * 8, 8)], rounds[2], d, where)

    def send4(d):
        t, where = plane_id(d)
        return remote(b_src.at[lax.rem(t, 8)], b_buf.at[:, pl.ds(q * 16, 16)], rounds[3], d, where)

    def start_all(send):
        @pl.loop(1, 16)
        def _(d):
            send(d).start()

    def arrive_all(send):
        @pl.loop(1, 16)
        def _(d):
            send(d).wait_recv()

    lane16 = lax.broadcasted_iota(jnp.int32, (16, 128), 1)

    loads[0].wait()
    loads[1].wait()
    brick = split(gas[0, pl.ds(1, BX)].reshape(BX * BY, BZ) - 1.0)
    turned = dot3((tz[0, :, 0:BZ], tz[1, :, 0:BZ]), brick, (((1,), (1,)), ((), ())))
    z_src[0] = turned[:, 0:128]
    z_src[1] = turned[:, 128:256]
    pl.semaphore_wait(barrier, 30)
    start_all(send1)
    z_buf[q] = z_src[:, pl.ds(pl.multiple_of(q * 16, 16), 16)]

    halos = (halo_send, halo_recv)
    above = {"hx": lax.rem(a + 1, 16)}
    below = {"hx": lax.rem(a + 15, 16)}
    right = {"hy": lax.rem(b + 1, 8)}
    left = {"hy": lax.rem(b + 7, 8)}
    other = {"ga": 1 - g}
    loads[2].wait()
    loads[3].wait()
    face_early = []
    for slot, (first, many) in enumerate(((0, 4), (5, 9))):
        rows = pl.ds(first, many)
        face_early.append(remote(gas.at[rows, BX], gas.at[rows, 0], halos, 2 * slot, above))
        face_early.append(remote(gas.at[rows, 1], gas.at[rows, BX + 1], halos, 2 * slot + 1, below))
    for face in face_early:
        face.start()
    loads[4].wait()
    loads[5].wait()
    lane8 = lax.broadcasted_iota(jnp.int32, (8, 128), 1)

    def cell_sound(p):
        return jnp.sqrt(gamma_gas * gas[4, p] / gas[0, p])

    @pl.loop(0, BX)
    def _(i):
        p = i + 1
        rho = gas[0, p]
        cooling = cool_rates[0] * gas[5, p]
        for s in range(1, 9):
            cooling = cooling + cool_rates[s] * gas[5 + s, p]
        stiffness = time_step * rho * cooling
        initial = press[i] / ((gamma_gas - 1.0) * rho)
        many = count[i]
        energy = initial
        for step in range(NEWTON):
            near = 1.0 + energy
            square = near * near
            top = (energy - initial) * square + stiffness * energy * energy * near
            bottom = square + stiffness * energy * (energy + 2.0)
            energy = jnp.where(many > step, energy - top / bottom, energy)
        gas[4, p] = (gamma_gas - 1.0) * rho * energy
        sound[p] = jnp.sqrt(gamma_gas * (gamma_gas - 1.0) * energy)
        tile = jnp.zeros((8, 128), f32)
        for f in range(15):
            field = gas[f, p] if f < 14 else sound[p]
            yp_src[0, i, f : f + 1, :] = field[BY - 1 : BY]
            yp_src[1, i, f : f + 1, :] = field[0:1]
            for j in range(4):
                moved = pltpu.roll(field[8 * j : 8 * j + 8], 32 * j + 2 * f + 1, 1)
                tile = jnp.where(lane8 // 2 == 16 * j + f, moved, tile)
        zp_src[i] = tile
        yp_src[0, i, 15:16, :] = jnp.zeros((1, 128), f32)
        yp_src[1, i, 15:16, :] = jnp.zeros((1, 128), f32)

    face_late = [
        remote(yp_src.at[0], yp_buf.at[0], halos, 6, right),
        remote(yp_src.at[1], yp_buf.at[1], halos, 7, left),
        remote(zp_src, zp_buf, halos, 8, other),
        remote(gas.at[4, BX], gas.at[4, 0], halos, 4, above),
        remote(gas.at[4, 1], gas.at[4, BX + 1], halos, 5, below),
    ]
    for face in face_late:
        face.start()

    loads[8].wait()
    total = lam[...] + lamz[q * 16 + a]
    inside = total < 0.0
    lam[...] = jnp.where(inside, (1.0 / (NX * NY * NZ)) / jnp.where(inside, total, -1.0), 0.0)

    row32 = lax.broadcasted_iota(jnp.int32, (BY, BZ), 0)
    lane32 = lax.broadcasted_iota(jnp.int32, (BY, BZ), 1)

    def hydro(i):
        p = i + 1

        def at(f, where):
            return gas[f, where] if f < 14 else sound[where]

        def sides(f, d):
            if d == 0:
                return at(f, p - 1), at(f, p + 1)
            field = at(f, p)
            if d == 1:
                lower = jnp.where(row32 == 0, yp_buf[0, i, f : f + 1, :], pltpu.roll(field, 1, 0))
                upper = jnp.where(
                    row32 == BY - 1, yp_buf[1, i, f : f + 1, :], pltpu.roll(field, BY - 1, 0)
                )
                return lower, upper
            tile = zp_buf[i]
            edge = jnp.concatenate(
                [pltpu.roll(tile, (BZ - 1 - 32 * j - 2 * f) % 128, 1) for j in range(4)], axis=0
            )
            lower = pltpu.roll(jnp.where(lane32 == BZ - 1, edge, field), 1, 1)
            upper = pltpu.roll(jnp.where(lane32 == 0, edge, field), BZ - 1, 1)
            return lower, upper

        rho = gas[0, p]
        vel = [gas[1 + k, p] for k in range(3)]
        cs = sound[p]
        keep = 1.0
        weights = []
        new_rho = 0.0
        new_energy = 0.0
        new_mom = [0.0, 0.0, 0.0]
        for d in range(3):
            rho_l, rho_u = sides(0, d)
            v_l, v_u = zip(*[sides(1 + k, d) for k in range(3)])
            p_l, p_u = sides(4, d)
            c_l, c_u = sides(14, d)
            here = jnp.abs(vel[d]) + cs
            w_l = jnp.maximum(here, jnp.abs(v_l[d]) + c_l)
            w_u = jnp.maximum(here, jnp.abs(v_u[d]) + c_u)
            b_l = half_step * (w_l + v_l[d])
            b_u = half_step * (w_u - v_u[d])
            a_l = b_l * rho_l
            a_u = b_u * rho_u
            keep = keep - half_step * (w_l + w_u)
            weights.append((a_l, a_u))
            new_rho = new_rho + (a_l + a_u)
            for k in range(3):
                new_mom[k] = new_mom[k] + (a_l * v_l[k] + a_u * v_u[k])
            new_mom[d] = new_mom[d] + half_step * (p_l - p_u)
            sq_l = v_l[0] * v_l[0] + v_l[1] * v_l[1] + v_l[2] * v_l[2]
            sq_u = v_u[0] * v_u[0] + v_u[1] * v_u[1] + v_u[2] * v_u[2]
            new_energy = new_energy + (
                0.5 * (a_l * sq_l + a_u * sq_u)
                + p_l * (1.5 * b_l + half_step * v_l[d])
                + p_u * (1.5 * b_u - half_step * v_u[d])
            )
        mass = keep * rho
        out[0, i] = new_rho + mass
        for k in range(3):
            out[1 + k, i] = new_mom[k] + mass * vel[k]
        sq = vel[0] * vel[0] + vel[1] * vel[1] + vel[2] * vel[2]
        out[4, i] = new_energy + keep * (1.5 * gas[4, p]) + 0.5 * mass * sq
        for s in range(5, 14):
            result = mass * gas[s, p]
            for d in range(3):
                lower, upper = sides(s, d)
                result = result + (weights[d][0] * lower + weights[d][1] * upper)
            out[s, i] = result

    loads[6].wait()
    arrive_all(send1)
    for hi in range(2):
        for xh in range(2):
            tiles = [z_buf[4 * hi + i, xh] + z_buf[8 + 4 * hi + i, xh] for i in range(4)]
            tiles = swap_chunks(tiles, lane16)
            for xl in range(4):
                u_buf[hi, pl.ds(4 * xh + xl, 16, stride=8), :] = tiles[xl]
    lines = split(jnp.concatenate([u_buf[0], u_buf[1]], axis=1))
    table_y = (ty[0], ty[1])
    y_src[...] = dot3(lines, table_y)
    start_all(send2)
    x_buf[pl.ds(pl.multiple_of(a * 8, 8), 8)] = y_src[pl.ds(pl.multiple_of(a * 8, 8), 8)]

    for face in face_late[0:3]:
        face.wait_recv()

    @pl.loop(1, 4)
    def _(i):
        hydro(i)

    loads[7].wait()
    arrive_all(send2)
    table_x = (tx[0], tx[1])
    waves = dot3(table_x, split(x_buf[...])) * lam[...]
    x_src[...] = dot3(table_x, split(waves))
    start_all(send3)
    w_buf[pl.ds(pl.multiple_of(a * 8, 8), 8)] = x_src[pl.ds(pl.multiple_of(a * 8, 8), 8)]

    @pl.loop(4, 7)
    def _(i):
        hydro(i)

    arrive_all(send3)
    back = dot3(split(w_buf[...]), table_y)
    v_buf[0] = back[:, 0:128]
    v_buf[1] = back[:, 128:256]
    for hi in range(2):
        for xh in range(2):
            tiles = [v_buf[hi, pl.ds(4 * xh + xl, 16, stride=8), :] for xl in range(4)]
            tiles = swap_chunks(tiles, lane16)
            for i in range(4):
                b_src[4 * hi + i, xh] = tiles[i]
    start_all(send4)
    b_buf[:, pl.ds(pl.multiple_of(q * 16, 16), 16)] = b_src[b]

    for face in face_early + face_late[3:5]:
        face.wait_recv()
    sound[0] = cell_sound(0)
    sound[BX + 1] = cell_sound(BX + 1)

    @pl.loop(0, 2)
    def _(i):
        hydro(i * (BX - 1))

    stores = [
        pltpu.make_async_copy(out.at[0], o_density, out_sem.at[0]),
        pltpu.make_async_copy(out.at[pl.ds(5, 9)], o_species, out_sem.at[1]),
    ]
    stores[0].start()
    stores[1].start()

    arrive_all(send4)
    table_back = (tz[0], tz[1])
    edges = []
    for xh in range(2):
        done = dot3(split(b_buf[xh].T), table_back)
        edges.append(done[:, BZ:])
        for xl in range(4):
            x = 4 * xh + xl
            pot[1 + x] = done[32 * xl : 32 * xl + 32, 0:BZ]
            py_src[0, x : x + 1, :] = done[32 * xl + 31 : 32 * xl + 32, 0:BZ]
            py_src[1, x : x + 1, :] = done[32 * xl : 32 * xl + 1, 0:BZ]
    pot_faces = [
        remote(pot.at[BX], pot.at[0], halos, 9, above),
        remote(pot.at[1], pot.at[BX + 1], halos, 10, below),
        remote(py_src.at[0], py_buf.at[0], halos, 11, right),
        remote(py_src.at[1], py_buf.at[1], halos, 12, left),
    ]
    for face in pot_faces:
        face.start()
    stores.append(pltpu.make_async_copy(pot.at[pl.ds(1, BX)], o_potential, out_sem.at[2]))
    stores[2].start()
    for face in pot_faces:
        face.wait_recv()
    for i in range(BX):
        here = pot[1 + i]
        edge = edges[i // 4][32 * (i % 4) : 32 * (i % 4) + 32]
        pull = [
            pot[i] - pot[i + 2],
            jnp.where(row32 == 0, py_buf[0, i : i + 1, :], pltpu.roll(here, 1, 0))
            - jnp.where(row32 == BY - 1, py_buf[1, i : i + 1, :], pltpu.roll(here, BY - 1, 0)),
            jnp.where(lane32 == 0, edge, pltpu.roll(here, 1, 1))
            - jnp.where(lane32 == BZ - 1, edge, pltpu.roll(here, BZ - 1, 1)),
        ]
        weight = half_step * gas[0, 1 + i]
        work = out[4, i]
        for k in range(3):
            push = weight * pull[k]
            out[1 + k, i] = out[1 + k, i] + push
            work = work + push * gas[1 + k, 1 + i]
        out[4, i] = work
    stores.append(pltpu.make_async_copy(out.at[pl.ds(1, 3)], o_momentum, out_sem.at[3]))
    stores.append(pltpu.make_async_copy(out.at[4], o_energy, out_sem.at[4]))
    stores[3].start()
    stores[4].start()

    for send in (send1, send2, send3, send4):

        @pl.loop(1, 16)
        def _(d):
            send(d).wait_send()

    for face in face_early + face_late + pot_faces:
        face.wait_send()
    for store in stores:
        store.wait()


def local(density, velocity, pressure, species, counts):
    brick = (BX, BY, BZ)
    shape = jax.ShapeDtypeStruct
    anywhere = pl.BlockSpec(memory_space=pl.ANY)
    vmem = pltpu.VMEM
    table_z, table_y, table_x, lam_xy, lam_z = tables()
    return pl.pallas_call(
        kernel,
        out_shape=(
            shape(brick, f32),
            shape((3,) + brick, f32),
            shape(brick, f32),
            shape((9,) + brick, f32),
            shape(brick, f32),
        ),
        in_specs=[anywhere] * 9 + [pl.BlockSpec(memory_space=pltpu.SMEM)],
        out_specs=(anywhere,) * 5,
        scratch_shapes=[
            vmem((14, BX + 2, BY, BZ), f32),
            vmem((BX + 2, BY, BZ), f32),
            vmem(brick, f32),
            vmem(brick, jnp.int32),
            vmem((2, NZ, 2 * BZ), bf16),
            vmem((2, NY, NY), bf16),
            vmem((2, NX, NX), bf16),
            vmem((NX, NY), f32),
            vmem((14,) + brick, f32),
            vmem((BX + 2, BY, BZ), f32),
            vmem((2, NZ, 128), f32),
            vmem((16, 2, 16, 128), f32),
            vmem((2, 128, 128), f32),
            vmem((128, 256), f32),
            vmem((128, 256), f32),
            vmem((128, 256), f32),
            vmem((128, 256), f32),
            vmem((2, 128, 128), f32),
            vmem((8, 2, 16, 128), f32),
            vmem((2, NZ, 128), f32),
            vmem((2, BX, 16, BZ), f32),
            vmem((2, BX, 16, BZ), f32),
            vmem((BX, 8, 128), f32),
            vmem((BX, 8, 128), f32),
            vmem((2, BX, BZ), f32),
            vmem((2, BX, BZ), f32),
            pltpu.SemaphoreType.DMA((9,)),
            pltpu.SemaphoreType.DMA((5,)),
            pltpu.SemaphoreType.DMA((4, 16)),
            pltpu.SemaphoreType.DMA((4, 16)),
            pltpu.SemaphoreType.DMA((13,)),
            pltpu.SemaphoreType.DMA((13,)),
        ],
        compiler_params=pltpu.CompilerParams(
            collective_id=0, has_side_effects=True, vmem_limit_bytes=40 * 1024 * 1024
        ),
        name="step",
    )(density, velocity, pressure, species, counts, table_z, table_y, table_x, lam_xy, lam_z)


def solution(mesh):
    in_specs = (
        P("hx", "hy", "ga"),
        P(None, "hx", "hy", "ga"),
        P("hx", "hy", "ga"),
        P(None, "hx", "hy", "ga"),
        P("hx", "hy", "ga"),
    )
    out_specs = (
        P("hx", "hy", "ga"),
        P(None, "hx", "hy", "ga"),
        P("hx", "hy", "ga"),
        P(None, "hx", "hy", "ga"),
        P("hx", "hy", "ga"),
    )
    return jax.shard_map(local, mesh=mesh, in_specs=in_specs, out_specs=out_specs, check_vma=False)
```

time: 213 us -> 64.5 us (0.30)
  Pallas kernels: 0 us -> 50.4 us
  starting transfers between devices: 45.7 us -> 0 us
  other arithmetic: 43.3 us -> 0 us
  local copies, waits for them, and re-layouts: 54.5 us -> 13.1 us
  waiting for transfers between devices: 37 us -> 0 us
  blocking collectives: 20.4 us -> 0 us
  matrix products: 9.23 us -> 0 us
    pallas_call x0 -> x1, Pallas kernels: none -> 50.4 us  [local(): pl.pallas_call(kernel, out_shape=(shape(brick, f32), shape((3,) + brick,...]
    all_to_all x6 -> x0, starting transfers between devices: 36.8 us -> none  [the longest x1 10.3 us: local(): lax.all_to_all(spectral, 'hx', split_axis=1, concat_axis=0, tiled=True)]
    all_to_all x6 -> x0, waiting for transfers between devices: 27 us -> none  [the longest x1 7.92 us: local(): lax.all_to_all(solved, 'hx', split_axis=0, concat_axis=1, tiled=True)]
    all_to_all x2 -> x0, blocking collectives: 20.4 us -> none  [the longest x1 11.9 us: column_pass(): lax.all_to_all(field, 'hy', split_axis=0, concat_axis=1, tiled=True)]
    sub x5 -> x0, other arithmetic: 16.6 us -> none  [the longest x3 9.85 us: face_flux(): 0.5 * (sides_data[0][1] + sides_data[1][1])]
    mul x14 -> x0, other arithmetic: 15 us -> none  [the longest x4 5.53 us: conserved(): density[None] * primitive[5:14]]
    slice x7 -> x0, local copies, waits for them, and re-layouts: 13.7 us -> none  [the longest x3 8.95 us: extended(): head = lax.slice_in_dim(cells, 0, width, axis=dim)]
    all_to_all x7 -> x0, local copies, waits for them, and re-layouts: 10.5 us -> none  [the longest x3 4.27 us: local(): lax.all_to_all(lax.all_to_all(solved, 'hx', split_axis=0, concat_axis=1,...]
  transfers between devices with their start and end apart: 12 -> 0, of which waited for: 9 -> 0; matrix products, arithmetic and copies ran while one was open for 12% -> 0% of each run, Pallas kernels for 0% -> 0%
where the time goes in v1:
time: 64.5 us; the launch traced here: 64.2 us
  Pallas kernels  50.4 us (78%)
  local copies, waits for them, and re-layouts  13.1 us (20%)
  between operations  0.66 us (1%)
    pallas_call x1, Pallas kernels, local(): pl.pallas_call(kernel, out_shape=(shape(brick, f32), shape((3,) + brick,...  50.4 us
    unnamed x25, local copies, waits for them, and re-layouts  13.1 us

profile of v1, /device:TPU:1, one launch (start us, length us, event | category | flops | bytes accessed | tf_op | source)
XLA Modules:
  0.0 64.2 jit_solution(4262344107526015455)
XLA Ops:
  0.6 0.0 copy-start
  0.6 1.3 %copy-done = f32[9,8,32,128]{3,2,1,0:T(8,128)S(1)} copy-done((f32[9,8,32,128]{3,2,1,0:T(8,128)S(1)}, f32[9,8,32,128]{3,2,1,0:T(8,128)}, u32[]{:S(2)}) %copy-start) | copy-done | bytes 1179672
  1.9 0.0 copy-start.1
  1.9 1.0 %copy-done.1 = bf16[2,2,256,256]{3,2,1,0:T(8,128)(2,1)S(1)} copy-done((bf16[2,2,256,256]{3,2,1,0:T(8,128)(2,1)S(1)}, bf16[2,2,256,256]{3,2,1,0:T(8,128)(2,1)}, u32[]{:S(2)}) %copy-start.1) | copy-done | bytes 524312
  2.9 0.0 copy-start.2
  2.9 1.0 %copy-done.2 = f32[3,8,32,128]{3,2,1,0:T(8,128)S(1)} copy-done((f32[3,8,32,128]{3,2,1,0:T(8,128)S(1)}, f32[3,8,32,128]{3,2,1,0:T(8,128)}, u32[]{:S(2)}) %copy-start.2) | copy-done | bytes 393240
  3.9 0.0 copy-start.3
  3.9 0.9 %copy-done.3 = bf16[2,256,256]{2,1,0:T(8,128)(2,1)S(1)} copy-done((bf16[2,256,256]{2,1,0:T(8,128)(2,1)S(1)}, bf16[2,256,256]{2,1,0:T(8,128)(2,1)}, u32[]{:S(2)}) %copy-start.3) | copy-done | bytes 262168
  4.9 0.0 copy-start.4
  4.9 0.9 %copy-done.4 = f32[8,32,128]{2,1,0:T(8,128)S(1)} copy-done((f32[8,32,128]{2,1,0:T(8,128)S(1)}, f32[8,32,128]{2,1,0:T(8,128)}, u32[]{:S(2)}) %copy-start.4) | copy-done | bytes 131096
  5.8 0.0 copy-start.5
  5.8 0.9 %copy-done.5 = f32[8,32,128]{2,1,0:T(8,128)S(1)} copy-done((f32[8,32,128]{2,1,0:T(8,128)S(1)}, f32[8,32,128]{2,1,0:T(8,128)}, u32[]{:S(2)}) %copy-start.5) | copy-done | bytes 131096
  6.7 0.0 copy-start.6
  6.7 0.9 %copy-done.6 = s32[8,32,128]{2,1,0:T(8,128)S(1)} copy-done((s32[8,32,128]{2,1,0:T(8,128)S(1)}, s32[8,32,128]{2,1,0:T(8,128)}, u32[]{:S(2)}) %copy-start.6) | copy-done | bytes 131096
  7.6 0.0 copy-start.7
  7.6 0.9 %copy-done.7 = f32[128,256]{1,0:T(8,128)S(1)} copy-done((f32[128,256]{1,0:T(8,128)S(1)}, f32[128,256]{1,0:T(8,128)}, u32[]{:S(2)}) %copy-start.7) | copy-done | bytes 131096
  8.5 0.8 %copy-done.8 = bf16[2,128,128]{2,1,0:T(8,128)(2,1)S(1)} copy-done((bf16[2,128,128]{2,1,0:T(8,128)(2,1)S(1)}, bf16[2,128,128]{2,1,0:T(8,128)(2,1)}, u32[]{:S(2)}) %copy-start.8) | copy-done | bytes 65560
  9.4 0.7 %copy-done.9 = f32[256]{0:T(256)S(1)} copy-done((f32[256]{0:T(256)S(1)}, f32[256]{0:T(256)}, u32[]{:S(2)}) %copy-start.9) | copy-done | bytes 1048
  10.0 50.4 %step.1 = (f32[8,32,128]{2,1,0:T(8,128)S(1)}, f32[3,8,32,128]{3,2,1,0:T(8,128)S(1)}, f32[8,32,128]{2,1,0:T(8,128)S(1)}, f32[9,8,32,128]{3,2,1,0:T(8,128)S(1)}, f32[8,32,128]{2,1,0:T(8,128)S(1)}) custom-call(f32[8,32,128]{2,1,0:T(8,128)S(1)} %copy-done.4, f32[3,8,32,128]{3,2,1,0:T(8,128)S(1)} %copy-done.2, f32[8,32,128]{2,1,0:T(8,128)S(1)} %copy-done.5, ...), custom_call_target="tpu_custom_call" | custom-call | tf_op jit(solution)/shard_map/step/pallas_call | solution.py:437
  60.4 0.7 %copy.20 = f32[8,32,128]{2,1,0:T(8,128)} copy(f32[8,32,128]{2,1,0:T(8,128)S(1)} %get-tuple-element.10) | data formatting | bytes 262144
  61.1 0.7 %copy.21 = f32[3,8,32,128]{3,2,1,0:T(8,128)} copy(f32[3,8,32,128]{3,2,1,0:T(8,128)S(1)} %get-tuple-element.11) | data formatting | bytes 786432
  61.8 0.7 %copy.22 = f32[8,32,128]{2,1,0:T(8,128)} copy(f32[8,32,128]{2,1,0:T(8,128)S(1)} %get-tuple-element.12) | data formatting | bytes 262144
  62.5 1.0 %copy.23 = f32[9,8,32,128]{3,2,1,0:T(8,128)} copy(f32[9,8,32,128]{3,2,1,0:T(8,128)S(1)} %get-tuple-element.13) | data formatting | bytes 2359296
  63.5 0.7 %copy.24 = f32[8,32,128]{2,1,0:T(8,128)} copy(f32[8,32,128]{2,1,0:T(8,128)S(1)} %get-tuple-element.14) | data formatting | bytes 262144
  (2 shorter events, 0.0 us)
Async XLA Ops:
  0.6 1.3 %copy-start = (f32[9,8,32,128]{3,2,1,0:T(8,128)S(1)}, f32[9,8,32,128]{3,2,1,0:T(8,128)}, u32[]{:S(2)}) copy-start(f32[9,8,32,128]{3,2,1,0:T(8,128)} %species.1) | copy-start | bytes 3538948
  1.9 1.0 %copy-start.1 = (bf16[2,2,256,256]{3,2,1,0:T(8,128)(2,1)S(1)}, bf16[2,2,256,256]{3,2,1,0:T(8,128)(2,1)}, u32[]{:S(2)}) copy-start(bf16[2,2,256,256]{3,2,1,0:T(8,128)(2,1)} %constant.10.clone.tz_in) | copy-start | bytes 1572868
  2.9 1.0 %copy-start.2 = (f32[3,8,32,128]{3,2,1,0:T(8,128)S(1)}, f32[3,8,32,128]{3,2,1,0:T(8,128)}, u32[]{:S(2)}) copy-start(f32[3,8,32,128]{3,2,1,0:T(8,128)} %velocity.1) | copy-start | bytes 1179652
  3.9 0.9 %copy-start.3 = (bf16[2,256,256]{2,1,0:T(8,128)(2,1)S(1)}, bf16[2,256,256]{2,1,0:T(8,128)(2,1)}, u32[]{:S(2)}) copy-start(bf16[2,256,256]{2,1,0:T(8,128)(2,1)} %constant.11.clone.ty_in) | copy-start | bytes 786436
  4.9 0.9 %copy-start.4 = (f32[8,32,128]{2,1,0:T(8,128)S(1)}, f32[8,32,128]{2,1,0:T(8,128)}, u32[]{:S(2)}) copy-start(f32[8,32,128]{2,1,0:T(8,128)} %density.1) | copy-start | bytes 393220
  5.8 0.9 %copy-start.5 = (f32[8,32,128]{2,1,0:T(8,128)S(1)}, f32[8,32,128]{2,1,0:T(8,128)}, u32[]{:S(2)}) copy-start(f32[8,32,128]{2,1,0:T(8,128)} %pressure.1) | copy-start | bytes 393220
  6.7 0.9 %copy-start.6 = (s32[8,32,128]{2,1,0:T(8,128)S(1)}, s32[8,32,128]{2,1,0:T(8,128)}, u32[]{:S(2)}) copy-start(s32[8,32,128]{2,1,0:T(8,128)} %counts.1) | copy-start | bytes 393220
  7.6 0.9 %copy-start.7 = (f32[128,256]{1,0:T(8,128)S(1)}, f32[128,256]{1,0:T(8,128)}, u32[]{:S(2)}) copy-start(f32[128,256]{1,0:T(8,128)} %constant.13.clone.lam_in) | copy-start | bytes 393220
  8.5 0.8 %copy-start.8 = (bf16[2,128,128]{2,1,0:T(8,128)(2,1)S(1)}, bf16[2,128,128]{2,1,0:T(8,128)(2,1)}, u32[]{:S(2)}) copy-start(bf16[2,128,128]{2,1,0:T(8,128)(2,1)} %constant.12.clone.tx_in) | copy-start | bytes 196612
  9.4 0.7 %copy-start.9 = (f32[256]{0:T(256)S(1)}, f32[256]{0:T(256)}, u32[]{:S(2)}) copy-start(f32[256]{0:T(256)} %constant.14.clone.lamz) | copy-start | bytes 3076

commit v2 on v1

--- a/solution.py
+++ b/solution.py
@@ -50,7 +50,13 @@
         edges[:, BZ - 1] = table_z[:, (first + BZ) % NZ]
         parts.append(halves(np.concatenate([table_z[:, first : first + BZ], edges], axis=1)))
     lam_xy = (eigen(NX)[:, None] + eigen(NY)[None, :]).astype(np.float32)
-    return np.stack(parts), halves(table_y), halves(cas_table(NX)), lam_xy, eigen(NZ).astype(np.float32)
+    table_x = cas_table(NX)
+    beyond = np.zeros((NX // BX, 8, NX))
+    for block in range(NX // BX):
+        beyond[block, 0:4:2] = table_x[(block * BX - 1) % NX]
+        beyond[block, 1:4:2] = table_x[(block * BX + BX) % NX]
+    table_x = np.concatenate([table_x, beyond.reshape(NX, NX)])
+    return np.stack(parts), halves(table_y), halves(table_x), lam_xy, eigen(NZ).astype(np.float32)
 
 
 def split(values):
@@ -81,16 +87,18 @@
 
 def kernel(
     density, velocity, pressure, species, counts, tz_in, ty_in, tx_in, lam_in, lamz,
-    o_density, o_momentum, o_energy, o_species, o_potential,
-    gas, sound, press, count, tz, ty, tx, lam, out, pot,
-    z_src, z_buf, u_buf, y_src, x_buf, x_src, w_buf, v_buf, b_src, b_buf,
-    yp_src, yp_buf, zp_src, zp_buf, py_src, py_buf,
+    o_density, o_momentum, o_energy, o_species, b_buf,
+    gas, sound, press, count, tz, ty, tx, lam, out,
+    z_src, z_buf, u_buf, y_src, x_buf, x_src, w_buf, v_buf, b_src,
+    yp_src, yp_buf, zp_src, zp_buf,
     in_sem, out_sem, send_sem, recv_sem, halo_send, halo_recv,
 ):
     a = lax.axis_index("hx")
     b = lax.axis_index("hy")
     g = lax.axis_index("ga")
     q = g * 8 + b
+    side = lax.rem(g + a, 2)
+    chunk = side * 8 + b
 
     loads = [
         (density, gas.at[0, pl.ds(1, BX)]),
@@ -109,18 +117,28 @@
 
     barrier = pltpu.get_barrier_semaphore()
 
-    def plane_id(offset):
-        t = lax.rem(q + offset, 16)
-        return t, {"hy": lax.rem(t, 8), "ga": t // 8}
-
-    def line_id(offset):
-        t = lax.rem(a + offset, 16)
-        return t, {"hx": t}
-
-    @pl.loop(1, 16)
-    def _(d):
-        pl.semaphore_signal(barrier, inc=1, device_id=plane_id(d)[1], device_id_type=MESH)
-        pl.semaphore_signal(barrier, inc=1, device_id=line_id(d)[1], device_id_type=MESH)
+    def outward(n, middle):
+        return middle + ((n + 1) // 2) * (2 * lax.rem(n, 2) - 1)
+
+    def plane_id(n):
+        t_b = lax.rem(b + outward(n // 2, 4), 8)
+        t_g = lax.rem(g + 1 + n, 2)
+        return t_b, t_g, {"hy": t_b, "ga": t_g}
+
+    def line_id(n):
+        t = lax.rem(a + outward(n, 8), 16)
+        return t, {"hx": t, "ga": lax.rem(side + t, 2)}
+
+    above = {"hx": lax.rem(a + 1, 16)}
+    below = {"hx": lax.rem(a + 15, 16)}
+
+    @pl.loop(0, 15)
+    def _(n):
+        pl.semaphore_signal(barrier, inc=1, device_id=plane_id(n)[2], device_id_type=MESH)
+        pl.semaphore_signal(barrier, inc=1, device_id=line_id(n)[1], device_id_type=MESH)
+
+    pl.semaphore_signal(barrier, inc=1, device_id=above, device_id_type=MESH)
+    pl.semaphore_signal(barrier, inc=1, device_id=below, device_id_type=MESH)
 
     def remote(src, dst, sems, slot, target):
         return pltpu.make_async_remote_copy(
@@ -130,31 +148,32 @@
 
     rounds = [(send_sem.at[r], recv_sem.at[r]) for r in range(4)]
 
-    def send1(d):
-        t, where = plane_id(d)
-        return remote(z_src.at[:, pl.ds(t * 16, 16)], z_buf.at[q], rounds[0], d, where)
-
-    def send2(d):
-        t, where = line_id(d)
-        return remote(y_src.at[pl.ds(t * 8, 8)], x_buf.at[pl.ds(a * 8, 8)], rounds[1], d, where)
-
-    def send3(d):
-        t, where = line_id(d)
-        return remote(x_src.at[pl.ds(t * 8, 8)], w_buf.at[pl.ds(a * 8, 8)], rounds[2], d, where)
-
-    def send4(d):
-        t, where = plane_id(d)
-        return remote(b_src.at[lax.rem(t, 8)], b_buf.at[:, pl.ds(q * 16, 16)], rounds[3], d, where)
+    def send1(n):
+        t_b, t_g, where = plane_id(n)
+        t = lax.rem(t_g + a, 2) * 8 + t_b
+        return remote(z_src.at[:, pl.ds(t * 16, 16)], z_buf.at[q], rounds[0], n, where)
+
+    def send2(n):
+        t, where = line_id(n)
+        return remote(y_src.at[pl.ds(t * 8, 8)], x_buf.at[pl.ds(a * 8, 8)], rounds[1], n, where)
+
+    def send3(n):
+        t, where = line_id(n)
+        return remote(x_src.at[pl.ds(t * 8, 8)], w_buf.at[pl.ds(a * 8, 8)], rounds[2], n, where)
+
+    def send4(n):
+        t_b, _, where = plane_id(n)
+        return remote(b_src.at[t_b], b_buf.at[:, pl.ds(chunk * 16, 16)], rounds[3], n, where)
 
     def start_all(send):
-        @pl.loop(1, 16)
-        def _(d):
-            send(d).start()
+        @pl.loop(0, 15)
+        def _(n):
+            send(n).start()
 
     def arrive_all(send):
-        @pl.loop(1, 16)
-        def _(d):
-            send(d).wait_recv()
+        @pl.loop(0, 15)
+        def _(n):
+            send(n).wait_recv()
 
     lane16 = lax.broadcasted_iota(jnp.int32, (16, 128), 1)
 
@@ -164,13 +183,11 @@
     turned = dot3((tz[0, :, 0:BZ], tz[1, :, 0:BZ]), brick, (((1,), (1,)), ((), ())))
     z_src[0] = turned[:, 0:128]
     z_src[1] = turned[:, 128:256]
-    pl.semaphore_wait(barrier, 30)
+    pl.semaphore_wait(barrier, 32)
     start_all(send1)
-    z_buf[q] = z_src[:, pl.ds(pl.multiple_of(q * 16, 16), 16)]
+    z_buf[q] = z_src[:, pl.ds(pl.multiple_of(chunk * 16, 16), 16)]
 
     halos = (halo_send, halo_recv)
-    above = {"hx": lax.rem(a + 1, 16)}
-    below = {"hx": lax.rem(a + 15, 16)}
     right = {"hy": lax.rem(b + 1, 8)}
     left = {"hy": lax.rem(b + 7, 8)}
     other = {"ga": 1 - g}
@@ -232,7 +249,7 @@
         face.start()
 
     loads[8].wait()
-    total = lam[...] + lamz[q * 16 + a]
+    total = lam[...] + lamz[chunk * 16 + a]
     inside = total < 0.0
     lam[...] = jnp.where(inside, (1.0 / (NX * NY * NZ)) / jnp.where(inside, total, -1.0), 0.0)
 
@@ -332,9 +349,11 @@
 
     loads[7].wait()
     arrive_all(send2)
-    table_x = (tx[0], tx[1])
-    waves = dot3(table_x, split(x_buf[...])) * lam[...]
-    x_src[...] = dot3(table_x, split(waves))
+    waves = dot3((tx[0, 0:NX], tx[1, 0:NX]), split(x_buf[...])) * lam[...]
+    solved = dot3((tx[0], tx[1]), split(waves))
+    x_src[:, 0:NY] = solved[0:NX]
+    row128 = lax.broadcasted_iota(jnp.int32, (NX, 128), 0)
+    x_src[:, NY:] = jnp.where(row128 % 8 < 2, solved[NX:, 0:128], solved[NX:, 128:NY])
     start_all(send3)
     w_buf[pl.ds(pl.multiple_of(a * 8, 8), 8)] = x_src[pl.ds(pl.multiple_of(a * 8, 8), 8)]
 
@@ -343,17 +362,42 @@
         hydro(i)
 
     arrive_all(send3)
-    back = dot3(split(w_buf[...]), table_y)
-    v_buf[0] = back[:, 0:128]
-    v_buf[1] = back[:, 128:256]
+    faces = w_buf[:, NY:]
+    faces = jnp.concatenate([faces, pltpu.roll(faces, NX - 2, 0)], axis=1)
+    back = dot3(split(jnp.concatenate([w_buf[:, 0:NY], faces], axis=0)), table_y)
     for hi in range(2):
+        v_buf[0, hi] = back[0:NX, 128 * hi : 128 * hi + 128]
+        v_buf[1, hi] = back[NX:, 128 * hi : 128 * hi + 128]
+
+    def line(kind, hi, row):
+        return v_buf[kind, hi, pl.ds(row, 16, stride=8), :]
+
+    spot = lane16 % 32
+    for hi in range(2):
+        rows_low = jnp.zeros((16, 128), f32)
+        rows_high = rows_low
         for xh in range(2):
-            tiles = [v_buf[hi, pl.ds(4 * xh + xl, 16, stride=8), :] for xl in range(4)]
+            tiles = [line(0, hi, 4 * xh + xl) for xl in range(4)]
+            outer = [line(0, 1 - hi, 4 * xh + xl) for xl in range(4)]
+            for xl in range(4):
+                x = 4 * xh + xl
+                low = jnp.where(
+                    lane16 < 32, pltpu.roll(outer[xl], 1 + x, 1), pltpu.roll(tiles[xl], 1 + x, 1)
+                )
+                high = jnp.where(
+                    lane16 >= 96, pltpu.roll(outer[xl], 96 + x, 1), pltpu.roll(tiles[xl], 96 + x, 1)
+                )
+                rows_low = jnp.where(spot == x, low, rows_low)
+                rows_high = jnp.where(spot == x, high, rows_high)
             tiles = swap_chunks(tiles, lane16)
             for i in range(4):
                 b_src[4 * hi + i, xh] = tiles[i]
+        tiles = swap_chunks([line(1, hi, 0), line(1, hi, 1), rows_low, rows_high], lane16)
+        for i in range(4):
+            b_src[4 * hi + i, 2] = tiles[i]
     start_all(send4)
-    b_buf[:, pl.ds(pl.multiple_of(q * 16, 16), 16)] = b_src[b]
+    own = pltpu.make_async_copy(b_src.at[b], b_buf.at[:, pl.ds(chunk * 16, 16)], out_sem.at[4])
+    own.start()
 
     for face in face_early + face_late[3:5]:
         face.wait_recv()
@@ -365,65 +409,93 @@
         hydro(i * (BX - 1))
 
     stores = [
+        own,
         pltpu.make_async_copy(out.at[0], o_density, out_sem.at[0]),
-        pltpu.make_async_copy(out.at[pl.ds(5, 9)], o_species, out_sem.at[1]),
+        pltpu.make_async_copy(out.at[pl.ds(1, 3)], o_momentum, out_sem.at[1]),
+        pltpu.make_async_copy(out.at[4], o_energy, out_sem.at[2]),
+        pltpu.make_async_copy(out.at[pl.ds(5, 9)], o_species, out_sem.at[3]),
     ]
-    stores[0].start()
-    stores[1].start()
-
+    for store in stores[1:]:
+        store.start()
+
+    for send in (send1, send2, send3, send4):
+
+        @pl.loop(0, 15)
+        def _(n):
+            send(n).wait_send()
+
+    for face in face_early + face_late:
+        face.wait_send()
+    for store in stores:
+        store.wait()
     arrive_all(send4)
-    table_back = (tz[0], tz[1])
+
+
+def finish(
+    density, velocity, density_in, momentum_in, energy_in, species_in, waves, tz_in,
+    o_density, o_momentum, o_energy, o_species, o_potential,
+    rho, vel, new_rho, mom, energy, frac, spec, tz, pot, load_sem, store_sem,
+):
+    loads = [
+        (waves, spec),
+        (tz_in.at[lax.axis_index("ga")], tz),
+        (density_in, new_rho),
+        (species_in, frac),
+        (density, rho),
+        (velocity, vel),
+        (momentum_in, mom),
+        (energy_in, energy),
+    ]
+    loads = [pltpu.make_async_copy(s, d, load_sem.at[i]) for i, (s, d) in enumerate(loads)]
+    stores = [
+        (new_rho, o_density),
+        (frac, o_species),
+        (pot.at[pl.ds(1, BX)], o_potential),
+        (mom, o_momentum),
+        (energy, o_energy),
+    ]
+    stores = [pltpu.make_async_copy(s, d, store_sem.at[i]) for i, (s, d) in enumerate(stores)]
+    for load in loads:
+        load.start()
+    loads[0].wait()
+    loads[1].wait()
+    table = (tz[0], tz[1])
     edges = []
     for xh in range(2):
-        done = dot3(split(b_buf[xh].T), table_back)
+        done = dot3(split(spec[xh].T), table)
         edges.append(done[:, BZ:])
         for xl in range(4):
-            x = 4 * xh + xl
-            pot[1 + x] = done[32 * xl : 32 * xl + 32, 0:BZ]
-            py_src[0, x : x + 1, :] = done[32 * xl + 31 : 32 * xl + 32, 0:BZ]
-            py_src[1, x : x + 1, :] = done[32 * xl : 32 * xl + 1, 0:BZ]
-    pot_faces = [
-        remote(pot.at[BX], pot.at[0], halos, 9, above),
-        remote(pot.at[1], pot.at[BX + 1], halos, 10, below),
-        remote(py_src.at[0], py_buf.at[0], halos, 11, right),
-        remote(py_src.at[1], py_buf.at[1], halos, 12, left),
-    ]
-    for face in pot_faces:
-        face.start()
-    stores.append(pltpu.make_async_copy(pot.at[pl.ds(1, BX)], o_potential, out_sem.at[2]))
+            pot[1 + 4 * xh + xl] = done[32 * xl : 32 * xl + 32, 0:BZ]
     stores[2].start()
-    for face in pot_faces:
-        face.wait_recv()
+    done = dot3(split(spec[2].T), (tz[0, :, 0:BZ], tz[1, :, 0:BZ]))
+    pot[0] = done[0:32]
+    pot[BX + 1] = done[32:64]
+    for i in range(2):
+        loads[2 + i].wait()
+        stores[i].start()
+    for load in loads[4:]:
+        load.wait()
+    row32 = lax.broadcasted_iota(jnp.int32, (BY, BZ), 0)
+    lane32 = lax.broadcasted_iota(jnp.int32, (BY, BZ), 1)
     for i in range(BX):
         here = pot[1 + i]
         edge = edges[i // 4][32 * (i % 4) : 32 * (i % 4) + 32]
         pull = [
             pot[i] - pot[i + 2],
-            jnp.where(row32 == 0, py_buf[0, i : i + 1, :], pltpu.roll(here, 1, 0))
-            - jnp.where(row32 == BY - 1, py_buf[1, i : i + 1, :], pltpu.roll(here, BY - 1, 0)),
+            jnp.where(row32 == 0, done[64 + i : 65 + i], pltpu.roll(here, 1, 0))
+            - jnp.where(row32 == BY - 1, done[96 + i : 97 + i], pltpu.roll(here, BY - 1, 0)),
             jnp.where(lane32 == 0, edge, pltpu.roll(here, 1, 1))
             - jnp.where(lane32 == BZ - 1, edge, pltpu.roll(here, BZ - 1, 1)),
         ]
-        weight = half_step * gas[0, 1 + i]
-        work = out[4, i]
+        weight = half_step * rho[i]
+        work = energy[i]
         for k in range(3):
             push = weight * pull[k]
-            out[1 + k, i] = out[1 + k, i] + push
-            work = work + push * gas[1 + k, 1 + i]
-        out[4, i] = work
-    stores.append(pltpu.make_async_copy(out.at[pl.ds(1, 3)], o_momentum, out_sem.at[3]))
-    stores.append(pltpu.make_async_copy(out.at[4], o_energy, out_sem.at[4]))
+            mom[k, i] = mom[k, i] + push
+            work = work + push * vel[k, i]
+        energy[i] = work
     stores[3].start()
     stores[4].start()
-
-    for send in (send1, send2, send3, send4):
-
-        @pl.loop(1, 16)
-        def _(d):
-            send(d).wait_send()
-
-    for face in face_early + face_late + pot_faces:
-        face.wait_send()
     for store in stores:
         store.wait()
 
@@ -433,16 +505,18 @@
     shape = jax.ShapeDtypeStruct
     anywhere = pl.BlockSpec(memory_space=pl.ANY)
     vmem = pltpu.VMEM
+    dma = pltpu.SemaphoreType.DMA
+    room = 58 * 1024 * 1024
     table_z, table_y, table_x, lam_xy, lam_z = tables()
-    return pl.pallas_call(
+    gas_shapes = (
+        shape(brick, f32),
+        shape((3,) + brick, f32),
+        shape(brick, f32),
+        shape((9,) + brick, f32),
+    )
+    *gas, waves = pl.pallas_call(
         kernel,
-        out_shape=(
-            shape(brick, f32),
-            shape((3,) + brick, f32),
-            shape(brick, f32),
-            shape((9,) + brick, f32),
-            shape(brick, f32),
-        ),
+        out_shape=gas_shapes + (shape((3, NZ, 128), f32),),
         in_specs=[anywhere] * 9 + [pl.BlockSpec(memory_space=pltpu.SMEM)],
         out_specs=(anywhere,) * 5,
         scratch_shapes=[
@@ -452,38 +526,55 @@
             vmem(brick, jnp.int32),
             vmem((2, NZ, 2 * BZ), bf16),
             vmem((2, NY, NY), bf16),
-            vmem((2, NX, NX), bf16),
+            vmem((2, 2 * NX, NX), bf16),
             vmem((NX, NY), f32),
             vmem((14,) + brick, f32),
-            vmem((BX + 2, BY, BZ), f32),
             vmem((2, NZ, 128), f32),
             vmem((16, 2, 16, 128), f32),
             vmem((2, 128, 128), f32),
-            vmem((128, 256), f32),
-            vmem((128, 256), f32),
-            vmem((128, 256), f32),
-            vmem((128, 256), f32),
-            vmem((2, 128, 128), f32),
-            vmem((8, 2, 16, 128), f32),
-            vmem((2, NZ, 128), f32),
+            vmem((128, NY), f32),
+            vmem((128, NY), f32),
+            vmem((128, NY + 128), f32),
+            vmem((128, NY + 128), f32),
+            vmem((2, 2, 128, 128), f32),
+            vmem((8, 3, 16, 128), f32),
             vmem((2, BX, 16, BZ), f32),
             vmem((2, BX, 16, BZ), f32),
             vmem((BX, 8, 128), f32),
             vmem((BX, 8, 128), f32),
-            vmem((2, BX, BZ), f32),
-            vmem((2, BX, BZ), f32),
-            pltpu.SemaphoreType.DMA((9,)),
-            pltpu.SemaphoreType.DMA((5,)),
-            pltpu.SemaphoreType.DMA((4, 16)),
-            pltpu.SemaphoreType.DMA((4, 16)),
-            pltpu.SemaphoreType.DMA((13,)),
-            pltpu.SemaphoreType.DMA((13,)),
+            dma((9,)),
+            dma((5,)),
+            dma((4, 15)),
+            dma((4, 15)),
+            dma((9,)),
+            dma((9,)),
         ],
         compiler_params=pltpu.CompilerParams(
-            collective_id=0, has_side_effects=True, vmem_limit_bytes=40 * 1024 * 1024
+            collective_id=0, has_side_effects=True, vmem_limit_bytes=room
         ),
         name="step",
     )(density, velocity, pressure, species, counts, table_z, table_y, table_x, lam_xy, lam_z)
+    return pl.pallas_call(
+        finish,
+        out_shape=gas_shapes + (shape(brick, f32),),
+        in_specs=[anywhere] * 8,
+        out_specs=(anywhere,) * 5,
+        scratch_shapes=[
+            vmem(brick, f32),
+            vmem((3,) + brick, f32),
+            vmem(brick, f32),
+            vmem((3,) + brick, f32),
+            vmem(brick, f32),
+            vmem((9,) + brick, f32),
+            vmem((3, NZ, 128), f32),
+            vmem((2, NZ, 2 * BZ), bf16),
+            vmem((BX + 2, BY, BZ), f32),
+            dma((8,)),
+            dma((5,)),
+        ],
+        compiler_params=pltpu.CompilerParams(vmem_limit_bytes=room),
+        name="finish",
+    )(density, velocity, *gas, waves, table_z)
 
 
 def solution(mesh):

time: 64.5 us -> 47.1 us (0.73)
  local copies, waits for them, and re-layouts: 13.1 us -> 0 us
  Pallas kernels: 50.4 us -> 46.3 us
    unnamed x25 -> x0, local copies, waits for them, and re-layouts: 13.1 us -> none
    pallas_call x1 -> x2, Pallas kernels: 50.4 us -> 46.3 us  [the longest x1 43.5 us: local(): pl.pallas_call(kernel, out_shape=gas_shapes + (shape((3, NZ, 128), f32),)...]
where the time goes in v2:
time: 47.1 us; the launch traced here: 46.9 us
  Pallas kernels  46.3 us (98%)
  between operations  0.64 us (1%)
    pallas_call x1, Pallas kernels, local(): pl.pallas_call(kernel, out_shape=gas_shapes + (shape((3, NZ, 128), f32),)...  43.5 us
    pallas_call x1, Pallas kernels, local(): pl.pallas_call(finish, out_shape=gas_shapes + (shape(brick, f32),), in_sp...  2.82 us

profile of v2, /device:TPU:1, one launch (start us, length us, event | category | flops | bytes accessed | tf_op | source)
XLA Modules:
  0.0 46.9 jit_solution(9605565958516411929)
XLA Ops:
  0.6 43.5 %step.1 = (f32[8,32,128]{2,1,0:T(8,128)}, f32[3,8,32,128]{3,2,1,0:T(8,128)}, f32[8,32,128]{2,1,0:T(8,128)}, f32[9,8,32,128]{3,2,1,0:T(8,128)}, f32[3,256,128]{2,1,0:T(8,128)}) custom-call(f32[8,32,128]{2,1,0:T(8,128)} %density.3, f32[3,8,32,128]{3,2,1,0:T(8,128)} %velocity.3, f32[8,32,128]{2,1,0:T(8,128)} %pressure.1, f32[9,8,32,128]{3,2,1,0:T(8,128)} %species.1, ...), custom_call_target="tpu_custom_call" | custom-call | tf_op jit(solution)/shard_map/step/pallas_call | solution.py:517
  44.1 2.8 %finish.1 = (f32[8,32,128]{2,1,0:T(8,128)}, f32[3,8,32,128]{3,2,1,0:T(8,128)}, f32[8,32,128]{2,1,0:T(8,128)}, f32[9,8,32,128]{3,2,1,0:T(8,128)}, f32[8,32,128]{2,1,0:T(8,128)}) custom-call(f32[8,32,128]{2,1,0:T(8,128)} %density.3, f32[3,8,32,128]{3,2,1,0:T(8,128)} %velocity.3, f32[8,32,128]{2,1,0:T(8,128)} %get-tuple-element.10.density_in, ...), custom_call_target="tpu_custom_call" | custom-call | tf_op jit(solution)/shard_map/finish/pallas_call | solution.py:557

commit v3 on v2

--- a/solution.py
+++ b/solution.py
@@ -34,13 +34,53 @@
     return np.stack([high, low])
 
 
-def eigen(extent):
-    waves = np.arange(extent).astype(np.float32)
-    return np.float32(2.0) * np.cos(np.float32(2.0 * np.pi / extent) * waves) - np.float32(2.0)
+def line_tables():
+    blocks = NX // BX
+    inner = BX - 1
+    lam_y = 4.0 * np.sin(np.pi * np.arange(NY) / NY) ** 2
+    lam_z = 4.0 * np.sin(np.pi * np.arange(NZ) / NZ) ** 2
+    center = 2.0 + lam_z[:, None] + lam_y[None, :]
+    factors = [1.0 / center]
+    for _ in range(inner - 1):
+        factors.append(1.0 / (center - factors[-1]))
+    near = factors[-1]
+    far = np.prod(np.stack(factors), axis=0)
+    sweep = np.stack(factors + [center], axis=0).reshape(BX, blocks, NZ // blocks, NY)
+    waves = np.arange(blocks)
+    values = (center - 2.0 * near)[:, None, :] - 2.0 * far[:, None, :] * np.cos(
+        2.0 * np.pi * waves / blocks
+    )[None, :, None]
+    values[0, 0, 0] = 1.0
+    inverse = 1.0 / (blocks * values)
+    bow = sum((x + 1) * (inner - x) for x in range(inner)) / 2.0
+    inverse[0, 0, 0] = bow / (BX * BX * blocks)
+    green = np.zeros((NZ, 48, NY // 2))
+    green[:, 0:16] = inverse[:, :, 0 : NY // 2]
+    green[:, 16:32] = inverse[:, :, NY // 2 :]
+    green[0, 32:34, 0] = -1.0 / (BX * blocks)
+    table = cas_table(blocks)
+    mix = np.zeros((48, blocks, 8))
+    spread = np.zeros((blocks, 8, 48))
+    for part in range(2):
+        rows = slice(16 * part, 16 * part + 16)
+        mix[rows, :, 2 * part] = table
+        mix[rows, :, 2 * part + 1] = np.roll(table, 1, axis=1)
+        spread[:, 2 * part, rows] = np.roll(table, 1, axis=0)
+        spread[:, 2 * part + 1, rows] = table
+    mix[32, :, 4] = 1.0
+    mix[33] = mix[0]
+    spread[:, 0:2, 32] = 1.0
+    spread[:, 4, 33] = 1.0
+    return (
+        halves(mix.reshape(48, 8 * blocks)),
+        halves(spread.reshape(8 * blocks, 48)),
+        green.astype(np.float32),
+        np.moveaxis(sweep, 0, 1).astype(np.float32),
+    )
 
 
 def tables():
-    table_y = cas_table(NY)
+    table_y = cas_table(NY) / 256.0
     table_z = cas_table(NZ)
     parts = []
     for rank in range(NZ // BZ):
@@ -49,14 +89,7 @@
         edges[:, 0] = table_z[:, (first - 1) % NZ]
         edges[:, BZ - 1] = table_z[:, (first + BZ) % NZ]
         parts.append(halves(np.concatenate([table_z[:, first : first + BZ], edges], axis=1)))
-    lam_xy = (eigen(NX)[:, None] + eigen(NY)[None, :]).astype(np.float32)
-    table_x = cas_table(NX)
-    beyond = np.zeros((NX // BX, 8, NX))
-    for block in range(NX // BX):
-        beyond[block, 0:4:2] = table_x[(block * BX - 1) % NX]
-        beyond[block, 1:4:2] = table_x[(block * BX + BX) % NX]
-    table_x = np.concatenate([table_x, beyond.reshape(NX, NX)])
-    return np.stack(parts), halves(table_y), halves(table_x), lam_xy, eigen(NZ).astype(np.float32)
+    return (np.stack(parts), halves(table_y)) + line_tables()
 
 
 def split(values):
@@ -86,10 +119,10 @@
 
 
 def kernel(
-    density, velocity, pressure, species, counts, tz_in, ty_in, tx_in, lam_in, lamz,
+    density, velocity, pressure, species, counts, tz_in, ty_in, mix_in, spread_in, green_in, sweep_in,
     o_density, o_momentum, o_energy, o_species, b_buf,
-    gas, sound, press, count, tz, ty, tx, lam, out,
-    z_src, z_buf, u_buf, y_src, x_buf, x_src, w_buf, v_buf, b_src,
+    gas, sound, press, count, tz, ty, mix, spread, green, sweep, out,
+    z_src, z_buf, u_buf, d_buf, y_src, x_buf, x_src, w_buf, b_src,
     yp_src, yp_buf, zp_src, zp_buf,
     in_sem, out_sem, send_sem, recv_sem, halo_send, halo_recv,
 ):
@@ -108,8 +141,10 @@
         (pressure, press),
         (counts, count),
         (ty_in, ty),
-        (tx_in, tx),
-        (lam_in, lam),
+        (mix_in, mix),
+        (spread_in, spread),
+        (green_in.at[chunk * 16 + a], green),
+        (sweep_in.at[chunk], sweep),
     ]
     loads = [pltpu.make_async_copy(s, d, in_sem.at[i]) for i, (s, d) in enumerate(loads)]
     for load in loads:
@@ -247,11 +282,6 @@
     ]
     for face in face_late:
         face.start()
-
-    loads[8].wait()
-    total = lam[...] + lamz[chunk * 16 + a]
-    inside = total < 0.0
-    lam[...] = jnp.where(inside, (1.0 / (NX * NY * NZ)) / jnp.where(inside, total, -1.0), 0.0)
 
     row32 = lax.broadcasted_iota(jnp.int32, (BY, BZ), 0)
     lane32 = lax.broadcasted_iota(jnp.int32, (BY, BZ), 1)
@@ -333,10 +363,37 @@
             tiles = [z_buf[4 * hi + i, xh] + z_buf[8 + 4 * hi + i, xh] for i in range(4)]
             tiles = swap_chunks(tiles, lane16)
             for xl in range(4):
-                u_buf[hi, pl.ds(4 * xh + xl, 16, stride=8), :] = tiles[xl]
-    lines = split(jnp.concatenate([u_buf[0], u_buf[1]], axis=1))
+                x = 4 * xh + xl
+                u_buf[16 * x : 16 * x + 16, 128 * hi : 128 * hi + 128] = tiles[xl]
     table_y = (ty[0], ty[1])
-    y_src[...] = dot3(lines, table_y)
+    d_buf[...] = dot3(split(u_buf[...]), table_y)
+
+    for load in loads[7:]:
+        load.wait()
+
+    def plane(x):
+        return d_buf[16 * x : 16 * x + 16, :]
+
+    def inside(before, after, mean):
+        values = []
+        carry = before
+        for x in range(BX - 1):
+            carry = carry + (mean - plane(x))
+            if x == BX - 2:
+                carry = carry + after
+            carry = carry * sweep[x]
+            values.append(carry)
+        for x in range(BX - 3, -1, -1):
+            values[x] = values[x] + sweep[x] * values[x + 1]
+        return values
+
+    values = inside(0.0, 0.0, 0.0)
+    last = values[BX - 2] - plane(BX - 1)
+    first = values[0]
+    whole = functools.reduce(lambda p, r: p + r, [v[:, 0:128] for v in values])
+    y_src[...] = jnp.zeros((128, 128), f32)
+    for r, row in enumerate((last[:, 0:128], first[:, 0:128], last[:, 128:], first[:, 128:], whole)):
+        y_src[pl.ds(r, 16, stride=8), :] = row
     start_all(send2)
     x_buf[pl.ds(pl.multiple_of(a * 8, 8), 8)] = y_src[pl.ds(pl.multiple_of(a * 8, 8), 8)]
 
@@ -347,13 +404,9 @@
     def _(i):
         hydro(i)
 
-    loads[7].wait()
     arrive_all(send2)
-    waves = dot3((tx[0, 0:NX], tx[1, 0:NX]), split(x_buf[...])) * lam[...]
-    solved = dot3((tx[0], tx[1]), split(waves))
-    x_src[:, 0:NY] = solved[0:NX]
-    row128 = lax.broadcasted_iota(jnp.int32, (NX, 128), 0)
-    x_src[:, NY:] = jnp.where(row128 % 8 < 2, solved[NX:, 0:128], solved[NX:, 128:NY])
+    waves = dot3((mix[0], mix[1]), split(x_buf[...])) * green[...]
+    x_src[...] = dot3((spread[0], spread[1]), split(waves))
     start_all(send3)
     w_buf[pl.ds(pl.multiple_of(a * 8, 8), 8)] = x_src[pl.ds(pl.multiple_of(a * 8, 8), 8)]
 
@@ -362,23 +415,28 @@
         hydro(i)
 
     arrive_all(send3)
-    faces = w_buf[:, NY:]
-    faces = jnp.concatenate([faces, pltpu.roll(faces, NX - 2, 0)], axis=1)
-    back = dot3(split(jnp.concatenate([w_buf[:, 0:NY], faces], axis=0)), table_y)
-    for hi in range(2):
-        v_buf[0, hi] = back[0:NX, 128 * hi : 128 * hi + 128]
-        v_buf[1, hi] = back[NX:, 128 * hi : 128 * hi + 128]
-
-    def line(kind, hi, row):
-        return v_buf[kind, hi, pl.ds(row, 16, stride=8), :]
+
+    def returned(r):
+        return w_buf[pl.ds(r, 16, stride=8), :]
+
+    before = jnp.concatenate([returned(0), returned(2)], axis=1)
+    own_plane = jnp.concatenate([returned(1), returned(3)], axis=1)
+    mean = returned(4)
+    mean = jnp.concatenate([mean, jnp.zeros_like(mean)], axis=1)
+    values = inside(before, own_plane, mean)
+    beyond = sweep[BX - 1] * own_plane - values[BX - 2] + (plane(BX - 1) - mean)
+    back = dot3(split(jnp.concatenate(values + [own_plane, before, beyond], axis=0)), table_y)
+
+    def line(hi, row):
+        return back[16 * row : 16 * row + 16, 128 * hi : 128 * hi + 128]
 
     spot = lane16 % 32
     for hi in range(2):
         rows_low = jnp.zeros((16, 128), f32)
         rows_high = rows_low
         for xh in range(2):
-            tiles = [line(0, hi, 4 * xh + xl) for xl in range(4)]
-            outer = [line(0, 1 - hi, 4 * xh + xl) for xl in range(4)]
+            tiles = [line(hi, 4 * xh + xl) for xl in range(4)]
+            outer = [line(1 - hi, 4 * xh + xl) for xl in range(4)]
             for xl in range(4):
                 x = 4 * xh + xl
                 low = jnp.where(
@@ -392,7 +450,7 @@
             tiles = swap_chunks(tiles, lane16)
             for i in range(4):
                 b_src[4 * hi + i, xh] = tiles[i]
-        tiles = swap_chunks([line(1, hi, 0), line(1, hi, 1), rows_low, rows_high], lane16)
+        tiles = swap_chunks([line(hi, 8), line(hi, 9), rows_low, rows_high], lane16)
         for i in range(4):
             b_src[4 * hi + i, 2] = tiles[i]
     start_all(send4)
@@ -507,7 +565,7 @@
     vmem = pltpu.VMEM
     dma = pltpu.SemaphoreType.DMA
     room = 58 * 1024 * 1024
-    table_z, table_y, table_x, lam_xy, lam_z = tables()
+    table_z, *others = tables()
     gas_shapes = (
         shape(brick, f32),
         shape((3,) + brick, f32),
@@ -517,7 +575,7 @@
     *gas, waves = pl.pallas_call(
         kernel,
         out_shape=gas_shapes + (shape((3, NZ, 128), f32),),
-        in_specs=[anywhere] * 9 + [pl.BlockSpec(memory_space=pltpu.SMEM)],
+        in_specs=[anywhere] * 11,
         out_specs=(anywhere,) * 5,
         scratch_shapes=[
             vmem((14, BX + 2, BY, BZ), f32),
@@ -526,23 +584,25 @@
             vmem(brick, jnp.int32),
             vmem((2, NZ, 2 * BZ), bf16),
             vmem((2, NY, NY), bf16),
-            vmem((2, 2 * NX, NX), bf16),
-            vmem((NX, NY), f32),
+            vmem((2, 48, 128), bf16),
+            vmem((2, 128, 48), bf16),
+            vmem((48, NY // 2), f32),
+            vmem((BX, 16, NY), f32),
             vmem((14,) + brick, f32),
             vmem((2, NZ, 128), f32),
             vmem((16, 2, 16, 128), f32),
-            vmem((2, 128, 128), f32),
             vmem((128, NY), f32),
             vmem((128, NY), f32),
-            vmem((128, NY + 128), f32),
-            vmem((128, NY + 128), f32),
-            vmem((2, 2, 128, 128), f32),
+            vmem((128, 128), f32),
+            vmem((128, 128), f32),
+            vmem((128, 128), f32),
+            vmem((128, 128), f32),
             vmem((8, 3, 16, 128), f32),
             vmem((2, BX, 16, BZ), f32),
             vmem((2, BX, 16, BZ), f32),
             vmem((BX, 8, 128), f32),
             vmem((BX, 8, 128), f32),
-            dma((9,)),
+            dma((11,)),
             dma((5,)),
             dma((4, 15)),
             dma((4, 15)),
@@ -553,7 +613,7 @@
             collective_id=0, has_side_effects=True, vmem_limit_bytes=room
         ),
         name="step",
-    )(density, velocity, pressure, species, counts, table_z, table_y, table_x, lam_xy, lam_z)
+    )(density, velocity, pressure, species, counts, table_z, *others)
     return pl.pallas_call(
         finish,
         out_shape=gas_shapes + (shape(brick, f32),),

time: 47.1 us -> 44 us (0.934)
  Pallas kernels: 46.3 us -> 43.2 us
    pallas_call x1, Pallas kernels: 43.5 us -> 40.4 us  [local(): pl.pallas_call(kernel, out_shape=gas_shapes + (shape((3, NZ, 128), f32),)...]
where the time goes in v3:
time: 44 us; the launch traced here: 43.8 us
  Pallas kernels  43.2 us (98%)
  between operations  0.64 us (1%)
    pallas_call x1, Pallas kernels, local(): pl.pallas_call(kernel, out_shape=gas_shapes + (shape((3, NZ, 128), f32),)...  40.4 us
    pallas_call x1, Pallas kernels, local(): pl.pallas_call(finish, out_shape=gas_shapes + (shape(brick, f32),), in_sp...  2.82 us

profile of v3, /device:TPU:1, one launch (start us, length us, event | category | flops | bytes accessed | tf_op | source)
XLA Modules:
  0.0 43.8 jit_solution(6554795182852777552)
XLA Ops:
  0.6 40.4 %step.1 = (f32[8,32,128]{2,1,0:T(8,128)}, f32[3,8,32,128]{3,2,1,0:T(8,128)}, f32[8,32,128]{2,1,0:T(8,128)}, f32[9,8,32,128]{3,2,1,0:T(8,128)}, f32[3,256,128]{2,1,0:T(8,128)}) custom-call(f32[8,32,128]{2,1,0:T(8,128)} %density.3, f32[3,8,32,128]{3,2,1,0:T(8,128)} %velocity.3, f32[8,32,128]{2,1,0:T(8,128)} %pressure.1, f32[9,8,32,128]{3,2,1,0:T(8,128)} %species.1, ...), custom_call_target="tpu_custom_call" | custom-call | tf_op jit(solution)/shard_map/step/pallas_call | solution.py:575
  41.0 2.8 %finish.1 = (f32[8,32,128]{2,1,0:T(8,128)}, f32[3,8,32,128]{3,2,1,0:T(8,128)}, f32[8,32,128]{2,1,0:T(8,128)}, f32[9,8,32,128]{3,2,1,0:T(8,128)}, f32[8,32,128]{2,1,0:T(8,128)}) custom-call(f32[8,32,128]{2,1,0:T(8,128)} %density.3, f32[3,8,32,128]{3,2,1,0:T(8,128)} %velocity.3, f32[8,32,128]{2,1,0:T(8,128)} %get-tuple-element.10.density_in, ...), custom_call_target="tpu_custom_call" | custom-call | tf_op jit(solution)/shard_map/finish/pallas_call | solution.py:617

commit v4 on v3

--- a/solution.py
+++ b/solution.py
@@ -229,11 +229,11 @@
     loads[2].wait()
     loads[3].wait()
     face_early = []
-    for slot, (first, many) in enumerate(((0, 4), (5, 9))):
+    for slot, (first, many) in enumerate(((0, 4), (4, 5), (9, 5))):
         rows = pl.ds(first, many)
-        face_early.append(remote(gas.at[rows, BX], gas.at[rows, 0], halos, 2 * slot, above))
-        face_early.append(remote(gas.at[rows, 1], gas.at[rows, BX + 1], halos, 2 * slot + 1, below))
-    for face in face_early:
+        face_early.append(remote(gas.at[rows, BX], gas.at[rows, 0], halos, 9 + 2 * slot, above))
+        face_early.append(remote(gas.at[rows, 1], gas.at[rows, BX + 1], halos, 10 + 2 * slot, below))
+    for face in face_early[0:2]:
         face.start()
     loads[4].wait()
     loads[5].wait()
@@ -277,8 +277,6 @@
         remote(yp_src.at[0], yp_buf.at[0], halos, 6, right),
         remote(yp_src.at[1], yp_buf.at[1], halos, 7, left),
         remote(zp_src, zp_buf, halos, 8, other),
-        remote(gas.at[4, BX], gas.at[4, 0], halos, 4, above),
-        remote(gas.at[4, 1], gas.at[4, BX + 1], halos, 5, below),
     ]
     for face in face_late:
         face.start()
@@ -395,6 +393,8 @@
     for r, row in enumerate((last[:, 0:128], first[:, 0:128], last[:, 128:], first[:, 128:], whole)):
         y_src[pl.ds(r, 16, stride=8), :] = row
     start_all(send2)
+    for face in face_early[2:4]:
+        face.start()
     x_buf[pl.ds(pl.multiple_of(a * 8, 8), 8)] = y_src[pl.ds(pl.multiple_of(a * 8, 8), 8)]
 
     for face in face_late[0:3]:
@@ -408,6 +408,8 @@
     waves = dot3((mix[0], mix[1]), split(x_buf[...])) * green[...]
     x_src[...] = dot3((spread[0], spread[1]), split(waves))
     start_all(send3)
+    for face in face_early[4:6]:
+        face.start()
     w_buf[pl.ds(pl.multiple_of(a * 8, 8), 8)] = x_src[pl.ds(pl.multiple_of(a * 8, 8), 8)]
 
     @pl.loop(4, 7)
@@ -457,7 +459,7 @@
     own = pltpu.make_async_copy(b_src.at[b], b_buf.at[:, pl.ds(chunk * 16, 16)], out_sem.at[4])
     own.start()
 
-    for face in face_early + face_late[3:5]:
+    for face in face_early:
         face.wait_recv()
     sound[0] = cell_sound(0)
     sound[BX + 1] = cell_sound(BX + 1)
@@ -606,8 +608,8 @@
             dma((5,)),
             dma((4, 15)),
             dma((4, 15)),
-            dma((9,)),
-            dma((9,)),
+            dma((15,)),
+            dma((15,)),
         ],
         compiler_params=pltpu.CompilerParams(
             collective_id=0, has_side_effects=True, vmem_limit_bytes=room

time: 44 us -> 40.5 us (0.920)
  Pallas kernels: 43.2 us -> 39.7 us
    pallas_call x1, Pallas kernels: 40.4 us -> 36.9 us  [local(): pl.pallas_call(kernel, out_shape=gas_shapes + (shape((3, NZ, 128), f32),)...]
where the time goes in v4:
time: 40.5 us; the launch traced here: 40.3 us
  Pallas kernels  39.7 us (98%)
  between operations  0.64 us (2%)
    pallas_call x1, Pallas kernels, local(): pl.pallas_call(kernel, out_shape=gas_shapes + (shape((3, NZ, 128), f32),)...  36.9 us
    pallas_call x1, Pallas kernels, local(): pl.pallas_call(finish, out_shape=gas_shapes + (shape(brick, f32),), in_sp...  2.82 us

profile of v4, /device:TPU:1, one launch (start us, length us, event | category | flops | bytes accessed | tf_op | source)
XLA Modules:
  0.0 40.3 jit_solution(4634386801321261031)
XLA Ops:
  0.6 36.9 %step.1 = (f32[8,32,128]{2,1,0:T(8,128)}, f32[3,8,32,128]{3,2,1,0:T(8,128)}, f32[8,32,128]{2,1,0:T(8,128)}, f32[9,8,32,128]{3,2,1,0:T(8,128)}, f32[3,256,128]{2,1,0:T(8,128)}) custom-call(f32[8,32,128]{2,1,0:T(8,128)} %density.3, f32[3,8,32,128]{3,2,1,0:T(8,128)} %velocity.3, f32[8,32,128]{2,1,0:T(8,128)} %pressure.1, f32[9,8,32,128]{3,2,1,0:T(8,128)} %species.1, ...), custom_call_target="tpu_custom_call" | custom-call | tf_op jit(solution)/shard_map/step/pallas_call | solution.py:577
  37.5 2.8 %finish.1 = (f32[8,32,128]{2,1,0:T(8,128)}, f32[3,8,32,128]{3,2,1,0:T(8,128)}, f32[8,32,128]{2,1,0:T(8,128)}, f32[9,8,32,128]{3,2,1,0:T(8,128)}, f32[8,32,128]{2,1,0:T(8,128)}) custom-call(f32[8,32,128]{2,1,0:T(8,128)} %density.3, f32[3,8,32,128]{3,2,1,0:T(8,128)} %velocity.3, f32[8,32,128]{2,1,0:T(8,128)} %get-tuple-element.10.density_in, ...), custom_call_target="tpu_custom_call" | custom-call | tf_op jit(solution)/shard_map/finish/pallas_call | solution.py:619

commit v5 on v4

--- a/solution.py
+++ b/solution.py
@@ -229,7 +229,7 @@
     loads[2].wait()
     loads[3].wait()
     face_early = []
-    for slot, (first, many) in enumerate(((0, 4), (4, 5), (9, 5))):
+    for slot, (first, many) in enumerate(((0, 1), (1, 6), (7, 7))):
         rows = pl.ds(first, many)
         face_early.append(remote(gas.at[rows, BX], gas.at[rows, 0], halos, 9 + 2 * slot, above))
         face_early.append(remote(gas.at[rows, 1], gas.at[rows, BX + 1], halos, 10 + 2 * slot, below))
@@ -278,8 +278,6 @@
         remote(yp_src.at[1], yp_buf.at[1], halos, 7, left),
         remote(zp_src, zp_buf, halos, 8, other),
     ]
-    for face in face_late:
-        face.start()
 
     row32 = lax.broadcasted_iota(jnp.int32, (BY, BZ), 0)
     lane32 = lax.broadcasted_iota(jnp.int32, (BY, BZ), 1)
@@ -393,16 +391,11 @@
     for r, row in enumerate((last[:, 0:128], first[:, 0:128], last[:, 128:], first[:, 128:], whole)):
         y_src[pl.ds(r, 16, stride=8), :] = row
     start_all(send2)
+    for face in face_late:
+        face.start()
     for face in face_early[2:4]:
         face.start()
     x_buf[pl.ds(pl.multiple_of(a * 8, 8), 8)] = y_src[pl.ds(pl.multiple_of(a * 8, 8), 8)]
-
-    for face in face_late[0:3]:
-        face.wait_recv()
-
-    @pl.loop(1, 4)
-    def _(i):
-        hydro(i)
 
     arrive_all(send2)
     waves = dot3((mix[0], mix[1]), split(x_buf[...])) * green[...]
@@ -412,9 +405,13 @@
         face.start()
     w_buf[pl.ds(pl.multiple_of(a * 8, 8), 8)] = x_src[pl.ds(pl.multiple_of(a * 8, 8), 8)]
 
-    @pl.loop(4, 7)
+    for face in face_late[0:3]:
+        face.wait_recv()
+
+    @pl.loop(1, 7)
     def _(i):
         hydro(i)
+
 
     arrive_all(send3)
 
@@ -511,8 +508,10 @@
         (new_rho, o_density),
         (frac, o_species),
         (pot.at[pl.ds(1, BX)], o_potential),
-        (mom, o_momentum),
-        (energy, o_energy),
+        (mom.at[:, pl.ds(0, 4)], o_momentum.at[:, pl.ds(0, 4)]),
+        (energy.at[pl.ds(0, 4)], o_energy.at[pl.ds(0, 4)]),
+        (mom.at[:, pl.ds(4, 4)], o_momentum.at[:, pl.ds(4, 4)]),
+        (energy.at[pl.ds(4, 4)], o_energy.at[pl.ds(4, 4)]),
     ]
     stores = [pltpu.make_async_copy(s, d, store_sem.at[i]) for i, (s, d) in enumerate(stores)]
     for load in loads:
@@ -554,8 +553,11 @@
             mom[k, i] = mom[k, i] + push
             work = work + push * vel[k, i]
         energy[i] = work
-    stores[3].start()
-    stores[4].start()
+        if i == 3:
+            stores[3].start()
+            stores[4].start()
+    stores[5].start()
+    stores[6].start()
     for store in stores:
         store.wait()
 
@@ -632,7 +634,7 @@
             vmem((2, NZ, 2 * BZ), bf16),
             vmem((BX + 2, BY, BZ), f32),
             dma((8,)),
-            dma((5,)),
+            dma((7,)),
         ],
         compiler_params=pltpu.CompilerParams(vmem_limit_bytes=room),
         name="finish",

time: 40.5 us -> 39.8 us (0.983)
  Pallas kernels: 39.7 us -> 39 us
    pallas_call x1, Pallas kernels: 36.9 us -> 36.2 us  [local(): pl.pallas_call(kernel, out_shape=gas_shapes + (shape((3, NZ, 128), f32),)...]
where the time goes in v5:
time: 39.8 us; the launch traced here: 39.7 us
  Pallas kernels  39 us (98%)
  between operations  0.64 us (2%)
    pallas_call x1, Pallas kernels, local(): pl.pallas_call(kernel, out_shape=gas_shapes + (shape((3, NZ, 128), f32),)...  36.2 us
    pallas_call x1, Pallas kernels, local(): pl.pallas_call(finish, out_shape=gas_shapes + (shape(brick, f32),), in_sp...  2.82 us

profile of v5, /device:TPU:1, one launch (start us, length us, event | category | flops | bytes accessed | tf_op | source)
XLA Modules:
  0.0 39.7 jit_solution(4524916911072925911)
XLA Ops:
  0.6 36.2 %step.1 = (f32[8,32,128]{2,1,0:T(8,128)}, f32[3,8,32,128]{3,2,1,0:T(8,128)}, f32[8,32,128]{2,1,0:T(8,128)}, f32[9,8,32,128]{3,2,1,0:T(8,128)}, f32[3,256,128]{2,1,0:T(8,128)}) custom-call(f32[8,32,128]{2,1,0:T(8,128)} %density.3, f32[3,8,32,128]{3,2,1,0:T(8,128)} %velocity.3, f32[8,32,128]{2,1,0:T(8,128)} %pressure.1, f32[9,8,32,128]{3,2,1,0:T(8,128)} %species.1, ...), custom_call_target="tpu_custom_call" | custom-call | tf_op jit(solution)/shard_map/step/pallas_call | solution.py:579
  36.8 2.8 %finish.1 = (f32[8,32,128]{2,1,0:T(8,128)}, f32[3,8,32,128]{3,2,1,0:T(8,128)}, f32[8,32,128]{2,1,0:T(8,128)}, f32[9,8,32,128]{3,2,1,0:T(8,128)}, f32[8,32,128]{2,1,0:T(8,128)}) custom-call(f32[8,32,128]{2,1,0:T(8,128)} %density.3, f32[3,8,32,128]{3,2,1,0:T(8,128)} %velocity.3, f32[8,32,128]{2,1,0:T(8,128)} %get-tuple-element.10.density_in, ...), custom_call_target="tpu_custom_call" | custom-call | tf_op jit(solution)/shard_map/finish/pallas_call | solution.py:621

commit v6 on v5

--- a/solution.py
+++ b/solution.py
@@ -186,7 +186,7 @@
     def send1(n):
         t_b, t_g, where = plane_id(n)
         t = lax.rem(t_g + a, 2) * 8 + t_b
-        return remote(z_src.at[:, pl.ds(t * 16, 16)], z_buf.at[q], rounds[0], n, where)
+        return remote(z_src.at[t], z_buf.at[q], rounds[0], n, where)
 
     def send2(n):
         t, where = line_id(n)
@@ -198,7 +198,7 @@
 
     def send4(n):
         t_b, _, where = plane_id(n)
-        return remote(b_src.at[t_b], b_buf.at[:, pl.ds(chunk * 16, 16)], rounds[3], n, where)
+        return remote(b_src.at[t_b], b_buf.at[chunk], rounds[3], n, where)
 
     def start_all(send):
         @pl.loop(0, 15)
@@ -216,11 +216,11 @@
     loads[1].wait()
     brick = split(gas[0, pl.ds(1, BX)].reshape(BX * BY, BZ) - 1.0)
     turned = dot3((tz[0, :, 0:BZ], tz[1, :, 0:BZ]), brick, (((1,), (1,)), ((), ())))
-    z_src[0] = turned[:, 0:128]
-    z_src[1] = turned[:, 128:256]
+    z_src[:, 0] = turned[:, 0:128].reshape(16, 16, 128)
+    z_src[:, 1] = turned[:, 128:256].reshape(16, 16, 128)
     pl.semaphore_wait(barrier, 32)
     start_all(send1)
-    z_buf[q] = z_src[:, pl.ds(pl.multiple_of(chunk * 16, 16), 16)]
+    z_buf[q] = z_src[chunk]
 
     halos = (halo_send, halo_recv)
     right = {"hy": lax.rem(b + 1, 8)}
@@ -453,7 +453,7 @@
         for i in range(4):
             b_src[4 * hi + i, 2] = tiles[i]
     start_all(send4)
-    own = pltpu.make_async_copy(b_src.at[b], b_buf.at[:, pl.ds(chunk * 16, 16)], out_sem.at[4])
+    own = pltpu.make_async_copy(b_src.at[b], b_buf.at[chunk], out_sem.at[4])
     own.start()
 
     for face in face_early:
@@ -521,12 +521,12 @@
     table = (tz[0], tz[1])
     edges = []
     for xh in range(2):
-        done = dot3(split(spec[xh].T), table)
+        done = dot3(split(spec[:, xh].reshape(NZ, 128).T), table)
         edges.append(done[:, BZ:])
         for xl in range(4):
             pot[1 + 4 * xh + xl] = done[32 * xl : 32 * xl + 32, 0:BZ]
     stores[2].start()
-    done = dot3(split(spec[2].T), (tz[0, :, 0:BZ], tz[1, :, 0:BZ]))
+    done = dot3(split(spec[:, 2].reshape(NZ, 128).T), (tz[0, :, 0:BZ], tz[1, :, 0:BZ]))
     pot[0] = done[0:32]
     pot[BX + 1] = done[32:64]
     for i in range(2):
@@ -578,7 +578,7 @@
     )
     *gas, waves = pl.pallas_call(
         kernel,
-        out_shape=gas_shapes + (shape((3, NZ, 128), f32),),
+        out_shape=gas_shapes + (shape((16, 3, 16, 128), f32),),
         in_specs=[anywhere] * 11,
         out_specs=(anywhere,) * 5,
         scratch_shapes=[
@@ -593,7 +593,7 @@
             vmem((48, NY // 2), f32),
             vmem((BX, 16, NY), f32),
             vmem((14,) + brick, f32),
-            vmem((2, NZ, 128), f32),
+            vmem((16, 2, 16, 128), f32),
             vmem((16, 2, 16, 128), f32),
             vmem((128, NY), f32),
             vmem((128, NY), f32),
@@ -630,7 +630,7 @@
             vmem((3,) + brick, f32),
             vmem(brick, f32),
             vmem((9,) + brick, f32),
-            vmem((3, NZ, 128), f32),
+            vmem((16, 3, 16, 128), f32),
             vmem((2, NZ, 2 * BZ), bf16),
             vmem((BX + 2, BY, BZ), f32),
             dma((8,)),

time: 39.8 us -> 39.8 us (level)
  no operation moved by 1% of the time
where the time goes in v6:
time: 39.8 us; the launch traced here: 39.7 us
  Pallas kernels  39 us (98%)
  between operations  0.64 us (2%)
    pallas_call x1, Pallas kernels, local(): pl.pallas_call(kernel, out_shape=gas_shapes + (shape((16, 3, 16, 128), f3...  36.2 us
    pallas_call x1, Pallas kernels, local(): pl.pallas_call(finish, out_shape=gas_shapes + (shape(brick, f32),), in_sp...  2.82 us

profile of v6, /device:TPU:1, one launch (start us, length us, event | category | flops | bytes accessed | tf_op | source)
XLA Modules:
  0.0 39.7 jit_solution(2763346771282123055)
XLA Ops:
  0.6 36.2 %step.1 = (f32[8,32,128]{2,1,0:T(8,128)}, f32[3,8,32,128]{3,2,1,0:T(8,128)}, f32[8,32,128]{2,1,0:T(8,128)}, f32[9,8,32,128]{3,2,1,0:T(8,128)}, f32[16,3,16,128]{3,2,1,0:T(8,128)}) custom-call(f32[8,32,128]{2,1,0:T(8,128)} %density.3, f32[3,8,32,128]{3,2,1,0:T(8,128)} %velocity.3, f32[8,32,128]{2,1,0:T(8,128)} %pressure.1, f32[9,8,32,128]{3,2,1,0:T(8,128)} %species.1, ...), custom_call_target="tpu_custom_call" | custom-call | tf_op jit(solution)/shard_map/step/pallas_call | solution.py:579
  36.8 2.8 %finish.1 = (f32[8,32,128]{2,1,0:T(8,128)}, f32[3,8,32,128]{3,2,1,0:T(8,128)}, f32[8,32,128]{2,1,0:T(8,128)}, f32[9,8,32,128]{3,2,1,0:T(8,128)}, f32[8,32,128]{2,1,0:T(8,128)}) custom-call(f32[8,32,128]{2,1,0:T(8,128)} %density.3, f32[3,8,32,128]{3,2,1,0:T(8,128)} %velocity.3, f32[8,32,128]{2,1,0:T(8,128)} %get-tuple-element.10.density_in, ...), custom_call_target="tpu_custom_call" | custom-call | tf_op jit(solution)/shard_map/finish/pallas_call | solution.py:621
